TPU v7x, 256 devices: a whole 4x4x8 slice. The times are simulated.
256 devices in a mesh: rep: 32 (over z_lo, y, core), shard: 8 (over z_hi, x).
Axes of the slice: x: 4, y: 4, z: 8 (z_hi: 2, z_lo: 4; z = z_hi * 4 + z_lo), core: 2. Of those that a mesh axis runs over, the one named last changes fastest.
Arguments:
- master_old: float32 [32, 8, 4608], P('shard'), may hold values from -0.875 to 0.875
- moment_one_old: float32 [32, 8, 4608], P('shard'), may hold values from -0.625 to 0.625
- moment_two_old: float32 [32, 8, 4608], P('shard'), may hold values from 0.002 to 0.05
- grads: bfloat16 [32, 8, 32, 8, 4608], P('rep', 'shard'), may hold values from -0.125 to 0.125
- old_order: int32 [32], replicated, may hold values from 0 to 31, as said below
- new_order: int32 [32], replicated, may hold values from 0 to 31, as said below
- step: int32 [1], replicated, may hold values from 1 to 7
Outputs:
- master_new: float32 [32, 16, 8, 4608], P('rep', 'shard')
- moment_one_new: float32 [32, 16, 8, 4608], P('rep', 'shard')
- moment_two_new: float32 [32, 16, 8, 4608], P('rep', 'shard')
- weights: bfloat16 [32, 32, 8, 4608], P('rep')
Inputs may be any that keep to these rules, and one draw needn't show every extreme that they name: old_order and new_order are permutations of the block ids. Of the 4 blocks in the old slots of one old member, at most 1 have their new slot with new members 2 s and 2 s + 1, for every s; this count is reached. `new_order`: a permutation of the block ids, drawn together with old_order.
All inputs are finite; a program needn't handle non-finite values.
Results may differ from a plain program's by a relative error of at most 0.0004.
Values may be sent and summed in bfloat16 or wider, within the bound.
A program may use at most 64 MiB of HBM per device.

v0:
```python
import jax
import jax.numpy as jnp
from jax import lax
from jax.sharding import PartitionSpec as P


def partner(array, axis, apart):
    return lax.ppermute(array, axis, [(i, i ^ 1 << apart) for i in range(lax.axis_size(axis))])


def adam_update(master, first, second, grad, step):
    count = step[0].astype(jnp.float32)
    first2 = 0.9 * first + 0.1 * grad
    second2 = 0.95 * second + 0.05 * grad * grad
    fix_one = 1.0 - jnp.power(jnp.float32(0.9), count)
    fix_two = 1.0 - jnp.power(jnp.float32(0.95), count)
    direction = first2 / fix_one / (jnp.sqrt(second2 / fix_two) + 1e-08)
    updated = master - 0.1 * (direction + 0.1 * master)
    return (updated, first2, second2)


def body(master_old, moment_one_old, moment_two_old, grads, old_order, new_order, step):
    groups = lax.axis_size("shard")
    shard_idx = lax.axis_index("shard")
    member_par = lax.axis_index("rep") % 2
    blocks = old_order.shape[0]
    new_count = blocks // (2 * groups)
    counting = jnp.arange(blocks, dtype=jnp.int32)
    old_slot_of = jnp.zeros((blocks,), jnp.int32).at[old_order].set(counting)
    new_slot_of = jnp.zeros((blocks,), jnp.int32).at[new_order].set(counting)
    my_start = (2 * shard_idx + member_par) * new_count
    my_blocks = lax.dynamic_slice_in_dim(new_order, my_start, new_count, 0)
    source = jnp.take(old_slot_of, my_blocks, axis=0)
    ordered = jnp.take(grads[0, 0], new_order, axis=0)
    summed = lax.psum(ordered.astype(jnp.float32), "rep")
    pair_grad = lax.psum_scatter(summed, "shard", scatter_dimension=0, tiled=True)
    grad = lax.dynamic_slice_in_dim(pair_grad, member_par * new_count, new_count, 0)
    whole = (
        lax.all_gather(master_old, "shard", axis=0, tiled=True),
        lax.all_gather(moment_one_old, "shard", axis=0, tiled=True),
        lax.all_gather(moment_two_old, "shard", axis=0, tiled=True),
    )
    master = jnp.take(whole[0], source, axis=0)
    first = jnp.take(whole[1], source, axis=0)
    second = jnp.take(whole[2], source, axis=0)
    updated, first2, second2 = adam_update(master, first, second, grad, step)
    own_half = updated.astype(jnp.bfloat16)
    other_half = partner(own_half, "rep", 0)
    lower = jnp.where(member_par == 0, own_half, other_half)
    upper = jnp.where(member_par == 0, other_half, own_half)
    paired = jnp.concatenate([lower, upper], axis=0)
    gathered = lax.all_gather(paired, "shard", axis=0, tiled=True)
    weights = jnp.take(gathered, new_slot_of, axis=0)
    return (updated[None], first2[None], second2[None], weights[None])


def solution(mesh):
    return jax.shard_map(
        body,
        mesh=mesh,
        in_specs=(
            P("shard", None, None),
            P("shard", None, None),
            P("shard", None, None),
            P("rep", "shard", None, None, None),
            P(),
            P(),
            P(),
        ),
        out_specs=(
            P("rep", "shard", None, None),
            P("rep", "shard", None, None),
            P("rep", "shard", None, None),
            P("rep", None, None, None),
        ),
        check_vma=False,
    )
```

profile of v0, /device:TPU:1, one launch (start us, length us, event | category | flops | bytes accessed | tf_op | source)
XLA Modules:
  0.0 853.8 jit_solution(2920333784293147112)
XLA Ops:
  7.2 0.0 copy-start
  7.2 0.0 reduce-scatter.2.cloned.1.call-start
  7.2 0.8 compare_select_fusion.1
  8.0 0.7 compare_and_fusion.1
  8.7 0.1 copy-done
  8.9 2.1 gather_fusion.3
  11.0 4.2 select_convert_fusion
  15.1 0.0 reduce-scatter.2.cloned.1.call-update
  15.1 0.0 copy-start.2
  15.2 0.0 copy-start.1
  15.2 0.0 all-gather.9.cloned.1.call-start
  15.2 0.7 all-gather.9.cloned.1.call-update
  15.9 0.0 all-gather.7.cloned.1.call-start
  16.0 0.7 all-gather.7.cloned.1.call-update
  16.6 0.0 all-gather.5.cloned.1.call-start
  16.7 0.5 all-gather.5.cloned.1.call-update
  17.2 0.0 all-reduce.2.cloned.1.call-start
  17.3 135.8 %reduce-scatter.2.cloned.1.call-done = f32[4,8,4608]{2,1,0:T(8,128)} async-done(((f32[32,8,4608]{2,1,0:T(8,128)}), f32[4,8,4608]{2,1,0:T(8,128)}) %reduce-scatter.2.cloned.1.call-update) | async-done | bytes 589840 | tf_op jit(solution)/shard_map/reduce_scatter | solution.py:36
  153.1 0.0 all-reduce.2.cloned.1.call-update
  153.1 0.0 all-gather.11.cloned.1.call-start
  153.2 0.0 copy-done.2
  154.0 0.7 scatter_custom_fusion
  154.6 0.0 copy-done.1
  154.7 0.1 compare_select_fusion.4
  154.7 0.6 gather_fusion
  155.4 0.1 compare_and_fusion.2
  155.5 112.1 %all-gather.9.cloned.1.call-done = f32[32,8,4608]{2,1,0:T(8,128)} async-done(((f32[4,8,4608]{2,1,0:T(8,128)}), f32[32,8,4608]{2,1,0:T(8,128)}) %all-gather.9.cloned.1.call-update) | async-done | bytes 4718608 | tf_op jit(solution)/shard_map/all_gather | solution.py:41
  267.6 2.9 gather_fusion.4
  270.5 109.7 %all-gather.7.cloned.1.call-done = f32[32,8,4608]{2,1,0:T(8,128)} async-done(((f32[4,8,4608]{2,1,0:T(8,128)}), f32[32,8,4608]{2,1,0:T(8,128)}) %all-gather.7.cloned.1.call-update) | async-done | bytes 4718608 | tf_op jit(solution)/shard_map/all_gather | solution.py:40
  380.2 2.9 gather_fusion.2
  383.1 109.5 %all-gather.5.cloned.1.call-done = f32[32,8,4608]{2,1,0:T(8,128)} async-done(((f32[4,8,4608]{2,1,0:T(8,128)}), f32[32,8,4608]{2,1,0:T(8,128)}) %all-gather.5.cloned.1.call-update) | async-done | bytes 4718608 | tf_op jit(solution)/shard_map/all_gather | solution.py:39
  492.6 2.9 gather_fusion.1
  495.5 260.2 %all-reduce.2.cloned.1.call-done = f32[4,8,4608]{2,1,0:T(8,128)} async-done(((f32[4,8,4608]{2,1,0:T(8,128)}), f32[4,8,4608]{2,1,0:T(8,128)}) %all-reduce.2.cloned.1.call-update) | async-done | bytes 589840 | tf_op jit(solution)/shard_map/psum | solution.py:35
  755.7 2.1 fusion.8
  757.8 2.9 collective-permute-start
  760.7 1.0 collective-permute-done
  761.7 0.7 pad_maximum_fusion
  762.5 0.0 all-gather.11.cloned.1.call-update
  762.5 0.7 scatter_custom_fusion.1
  763.2 76.6 %all-gather.11.cloned.1.call-done = bf16[32,8,4608]{2,1,0:T(8,128)(2,1)} async-done(((bf16[4,8,4608]{2,1,0:T(8,128)(2,1)}), bf16[32,8,4608]{2,1,0:T(8,128)(2,1)}) %all-gather.11.cloned.1.call-update) | async-done | bytes 2359312 | tf_op jit(solution)/shard_map/all_gather | solution.py:52
  839.9 3.8 gather_fusion.5
  843.6 3.3 select_bitcast_fusion
  (10 shorter events, 0.1 us)
Async XLA Ops:
  7.2 1.7 copy-start
  7.2 145.9 %reduce-scatter.2.cloned.1.call-start = ((), (), s32[]{:S(2)}) async-start(), calls=%async_computation.5 | async-start | bytes 5308416 | tf_op jit(solution)/shard_map/reduce_scatter | solution.py:36
  15.1 138.0 %copy-start.2 = (s32[32]{0:T(128)S(1)}, s32[32]{0:T(128)}, u32[]{:S(2)}) copy-start(s32[32]{0:T(128)} %param.15) | copy-start | bytes 388
  15.2 139.5 %copy-start.1 = (s32[32]{0:T(128)S(1)}, s32[32]{0:T(128)}, u32[]{:S(2)}) copy-start(s32[32]{0:T(128)} %param.16) | copy-start | bytes 388
  15.2 252.5 %all-gather.9.cloned.1.call-start = ((), (), s32[]{:S(2)}) async-start(), calls=%async_computation.3 | async-start | bytes 5308416 | tf_op jit(solution)/shard_map/all_gather | solution.py:41
  15.9 364.3 %all-gather.7.cloned.1.call-start = ((), (), s32[]{:S(2)}) async-start(), calls=%async_computation.2 | async-start | bytes 5308416 | tf_op jit(solution)/shard_map/all_gather | solution.py:40
  16.6 476.0 %all-gather.5.cloned.1.call-start = ((), (), s32[]{:S(2)}) async-start(), calls=%async_computation.1 | async-start | bytes 5308416 | tf_op jit(solution)/shard_map/all_gather | solution.py:39
  17.2 738.5 %all-reduce.2.cloned.1.call-start = ((), (), s32[]{:S(2)}) async-start(), calls=%async_computation.6 | async-start | bytes 1179648 | tf_op jit(solution)/shard_map/psum | solution.py:35
  153.1 686.7 %all-gather.11.cloned.1.call-start = ((), (), s32[]{:S(2)}) async-start(), calls=%async_computation.4 | async-start | bytes 2654208 | tf_op jit(solution)/shard_map/all_gather | solution.py:52
  757.8 3.9 collective-permute-start
Sparse Core Ops, SparseCore 0:
  15.3 137.8 reduce-scatter.1
  156.0 111.5 all-gather.8
  270.6 109.5 all-gather.6
  383.0 109.5 all-gather.4
  495.3 260.3 all-reduce.1
  762.6 77.1 all-gather.10
where the time goes:
time: 854 us
  waiting for transfers between devices  807 us (94%)
  local copies, waits for them, and re-layouts  16.7 us (2%)
  between operations  15 us (2%)
  other arithmetic  12 us (1%)
    psum x1, waiting for transfers between devices, body(): summed = lax.psum(ordered.astype(jnp.float32), 'rep')  260 us
    reduce_scatter x1, waiting for transfers between devices, body(): lax.psum_scatter(summed, 'shard', scatter_dimension=0, tiled=True)  136 us
    all_gather x1, waiting for transfers between devices, body(): lax.all_gather(moment_two_old, 'shard', axis=0, tiled=True)  112 us
    all_gather x1, waiting for transfers between devices, body(): lax.all_gather(moment_one_old, 'shard', axis=0, tiled=True)  110 us
    all_gather x1, waiting for transfers between devices, body(): lax.all_gather(master_old, 'shard', axis=0, tiled=True)  110 us
    all_gather x1, waiting for transfers between devices, body(): gathered = lax.all_gather(paired, 'shard', axis=0, tiled=True)  76.6 us
  transfers between devices with their start and end apart: 7, of which 7 were waited for; matrix products, arithmetic and copies ran while one was open for 1% of the time, Pallas kernels for 0%

commit v1 on v0

v1 whole, which is shorter than its diff:
```python
import functools

import jax
import jax.numpy as jnp
import numpy as np
from jax import lax
from jax.experimental import pallas as pl
from jax.experimental.pallas import tpu as pltpu
from jax.sharding import PartitionSpec as P

MESH = pl.DeviceIdType.MESH
LANES = 128
F32 = jnp.float32
BF16 = jnp.bfloat16


def power(base, count):
    out = jnp.float32(1.0)
    for bit in range(11):
        factor = np.float32(float(base) ** (1 << bit))
        taken = lax.rem(lax.shift_right_logical(count, jnp.int32(bit)), jnp.int32(2)) == 1
        out = jnp.where(taken, out * factor, out)
    return jnp.where(count >= 2048, jnp.float32(0.0), out)


def kernel(
    dims,
    old_ref, new_ref, step_ref, grads, master, first, second,
    master_out, first_out, second_out, weights_out,
    own, sib, chip, state, state_out, cand,
    send_a, send_b, recv1_a, recv1_b, part_a, part_b, recv2_a, recv2_b,
    half_sum, recv3, result, result_z, other_z, pair, pairs, gathered, ordered,
    send_sem, recv_sem, local_sem,
):
    nx, ny, nzh, nzl, tiles, stop = dims
    nz, ns = nzh * nzl, nzh * nx
    half = tiles * LANES
    part = half // 2
    width = -(-tiles // nzl) * LANES
    starts = [(k * tiles // nzl) * LANES for k in range(nzl + 1)]

    rep, shard = lax.axis_index("rep"), lax.axis_index("shard")
    core = lax.rem(rep, 2)
    y = lax.rem(lax.div(rep, 2), ny)
    zl = lax.div(rep, 2 * ny)
    x, zh = lax.rem(shard, nx), lax.div(shard, nx)
    z = zh * nzl + zl

    def device(x=x, y=y, zh=zh, zl=zl, core=core):
        return ((zl * ny + y) * 2 + core, zh * nx + x)

    def ahead(value, by, size):
        return lax.rem(value + by, size)

    def piece(k):
        return pl.multiple_of(lax.div(k * tiles, nzl) * LANES, LANES)

    count = {"remote": 0, "local": 0}
    sent = []

    def remote(src, dst, to):
        k = count["remote"]
        count["remote"] += 1
        copy = pltpu.make_async_remote_copy(
            src_ref=src, dst_ref=dst, send_sem=send_sem.at[k], recv_sem=recv_sem.at[k],
            device_id=to, device_id_type=MESH,
        )
        copy.start()
        sent.append(copy)
        return copy

    def local(src, dst):
        k = count["local"]
        count["local"] += 1
        copy = pltpu.make_async_copy(src, dst, local_sem.at[k])
        copy.start()
        return copy

    far = lambda n: sorted(range(1, n), key=lambda d: -min(d, n - d))

    mine = pl.multiple_of(core * half, LANES)
    theirs = pl.multiple_of((1 - core) * half, LANES)
    loads = [local(grads.at[:, pl.ds(mine + h * part, part)], own.at[h]) for h in range(2)]
    spot = pl.ds(mine + piece(zl), width)
    state_loads = [local(ref.at[:, :, spot], state.at[k]) for k, ref in enumerate((master, first, second))]

    partners = [device(core=1 - core)]
    partners += [device(x=ahead(x, d, nx)) for d in range(1, nx)]
    partners += [device(y=ahead(y, d, ny)) for d in range(1, ny)]
    for d in range(1, nz):
        other = ahead(z, d, nz)
        partners.append(device(zh=lax.div(other, nzl), zl=lax.rem(other, nzl)))
    for e in range(1, nzh):
        partners += [device(x=ahead(x, d, nx), zh=ahead(zh, e, nzh)) for d in range(1, nx)]
    barrier = pltpu.get_barrier_semaphore()
    for partner in partners:
        pl.semaphore_signal(barrier, inc=1, device_id=partner, device_id_type=MESH)
    pl.semaphore_wait(barrier, len(partners))

    swaps = [
        remote(grads.at[:, pl.ds(theirs + h * part, part)], sib.at[h], device(core=1 - core))
        for h in range(2)
    ]

    for copy in state_loads:
        copy.wait()
    moves = {}
    for e in range(nzh):
        for d in range(nx):
            to_x, to_zh = ahead(x, d, nx), ahead(zh, e, nzh)
            wanted = new_ref[(to_zh * nx + to_x) * ny + y]
            pick = jnp.int32(0)
            for j in range(1, ny):
                pick = jnp.where(old_ref[shard * ny + j] == wanted, jnp.int32(j), pick)
            slot = e * nx + d
            target = cand if slot == 0 else state_out
            for k in range(3):
                target[slot, k] = state[k, pick]
            if slot:
                moves[slot] = remote(state_out.at[slot], cand.at[slot], device(x=to_x, zh=to_zh))

    def chip_sum(h):
        def add(i, carry):
            rows = pl.ds(pl.multiple_of(i * 16, 16), 16)
            both = own[h, rows, :].astype(F32) + sib[h, rows, :].astype(F32)
            chip[h, 2 * i] = both[:8]
            chip[h, 2 * i + 1] = both[8:]
            return carry

        lax.fori_loop(0, ns * ny // 2, add, 0)

    def order(h, buffer, lead, along_x):
        for inner in range(ny if along_x else nx):
            for e in range(nzh):
                to_x, to_y = (lead, inner) if along_x else (inner, lead)
                buffer[lead, inner, e] = chip[h, new_ref[(e * nx + to_x) * ny + to_y]]

    loads[0].wait()
    swaps[0].wait_recv()
    chip_sum(0)
    first_a = {}
    for d in far(nx) + [0]:
        to = ahead(x, d, nx)
        order(0, send_a, to, True)
        if d:
            first_a[d] = remote(send_a.at[to], recv1_a.at[d - 1], device(x=to))
    loads[1].wait()
    swaps[1].wait_recv()
    chip_sum(1)
    first_b = {}
    for d in far(ny) + [0]:
        to = ahead(y, d, ny)
        order(1, send_b, to, False)
        if d:
            first_b[d] = remote(send_b.at[to], recv1_b.at[d - 1], device(y=to))

    for d in range(1, nx):
        first_a[d].wait_recv()
    second_a = {}
    for d in far(ny) + [0]:
        to = ahead(y, d, ny)
        for e in range(nzh):
            total = send_a[x, to, e]
            for q in range(nx - 1):
                total = total + recv1_a[q, to, e]
            part_a[to, e] = total
        if d:
            second_a[d] = remote(part_a.at[to], recv2_a.at[d - 1], device(y=to))
    for d in range(1, ny):
        first_b[d].wait_recv()
    second_b = {}
    for d in far(nx) + [0]:
        to = ahead(x, d, nx)
        for e in range(nzh):
            total = send_b[y, to, e]
            for q in range(ny - 1):
                total = total + recv1_b[q, to, e]
            part_b[to, e] = total
        if d:
            second_b[d] = remote(part_b.at[to], recv2_b.at[d - 1], device(x=to))
    for d in range(1, ny):
        second_a[d].wait_recv()
    for e in range(nzh):
        total = part_a[y, e]
        for q in range(ny - 1):
            total = total + recv2_a[q, e]
        half_sum[e, :, :part] = total
    for d in range(1, nx):
        second_b[d].wait_recv()
    for e in range(nzh):
        total = part_b[x, e]
        for q in range(nx - 1):
            total = total + recv2_b[q, e]
        half_sum[e, :, part:] = total

    third = {}
    for d in far(nz):
        other = ahead(z, d, nz)
        to_zh, to_zl = lax.div(other, nzl), lax.rem(other, nzl)
        third[d] = remote(
            half_sum.at[to_zh, :, pl.ds(piece(to_zl), width)], recv3.at[d - 1], device(zh=to_zh, zl=to_zl)
        )

    wanted = new_ref[shard * ny + y]
    pick = jnp.int32(0)
    for e in range(nzh):
        for d in range(nx):
            slot = e * nx + d
            if slot:
                moves[slot].wait_recv()
                from_x, from_zh = ahead(x, nx - d, nx), ahead(zh, nzh - e, nzh)
                for j in range(ny):
                    match = old_ref[(from_zh * nx + from_x) * ny + j] == wanted
                    pick = jnp.where(match, jnp.int32(slot), pick)
    t = step_ref[0]
    fix_one = 1.0 - power(0.9, t)
    fix_two = 1.0 - power(0.95, t)

    for d in range(1, nz):
        third[d].wait_recv()
    grad = half_sum[zh, :, pl.ds(piece(zl), width)]
    for q in range(nz - 1):
        grad = grad + recv3[q]
    weight = cand[pick, 0]
    moment_one = 0.9 * cand[pick, 1] + 0.1 * grad
    moment_two = 0.95 * cand[pick, 2] + 0.05 * grad * grad
    direction = moment_one / fix_one / (jnp.sqrt(moment_two / fix_two) + 1e-08)
    result[0] = weight - 0.1 * (direction + 0.1 * weight)
    result[1] = moment_one
    result[2] = moment_two

    along = {}
    for e in range(nzh - 1, -1, -1):
        for d in far(nzl) + [0]:
            to = ahead(zl, d, nzl)
            if e:
                along[e, d] = remote(result.at[0], other_z.at[e - 1, zl], device(zh=ahead(zh, e, nzh), zl=to))
            elif d:
                along[e, d] = remote(result, result_z.at[zl], device(zl=to))
    for k in range(3):
        result_z[zl, k] = result[k]
    for copy in along.values():
        copy.wait_recv()
    for k in range(nzl):
        span = starts[k + 1] - starts[k]
        columns = slice(starts[k], starts[k + 1])
        for a in range(3):
            pair[a, :, columns] = result_z[k, a, :, :span]
        same = result_z[k, 0, :, :span]
        rows = []
        for e in range(nzh):
            value = same
            for q in range(1, nzh):
                value = jnp.where(ahead(zh, nzh - q, nzh) == e, other_z[q - 1, k, :, :span], value)
            rows.append(value)
        gathered[x, y, :, columns] = jnp.concatenate(rows, axis=0).astype(BF16)

    over_y = {}
    for d in far(ny):
        over_y[d] = remote(gathered.at[x, y], gathered.at[x, y], device(y=ahead(y, d, ny)))
    pair_y = {}
    for d in far(ny):
        pair_y[d] = remote(pair, pairs.at[y], device(y=ahead(y, d, ny)))
    for a in range(3):
        pairs[y, a] = pair[a]
    for d in range(1, ny):
        over_y[d].wait_recv()

    over_x = {}
    for d in far(nx):
        over_x[d] = remote(gathered.at[x], gathered.at[x], device(x=ahead(x, d, nx)))

    slots = []
    for b in range(ns * ny):
        slot = jnp.int32(0)
        for k in range(1, ns * ny):
            slot = jnp.where(new_ref[k] == b, jnp.int32(k), slot)
        slots.append(slot)
    for d in range(1, ny):
        pair_y[d].wait_recv()
    nb = ny // 2
    outs = []
    for a, ref in enumerate((master_out, first_out, second_out)):
        place = ref.at[:, :, pl.ds(mine, half)]
        outs.append(local(pairs.at[pl.ds(core * nb, nb), a], place))
        remote(pairs.at[pl.ds((1 - core) * nb, nb), a], place, device(core=1 - core))

    for d in range(1, nx):
        over_x[d].wait_recv()
    for i in range(ns * ny // 2):
        rows = []
        for b in (2 * i, 2 * i + 1):
            slot = slots[b]
            at_y, at_x = lax.rem(slot, ny), lax.rem(lax.div(slot, ny), nx)
            at_zh = lax.div(slot, ny * nx)
            block = gathered[at_x, at_y].astype(F32)
            value = block[:8]
            for e in range(1, nzh):
                value = jnp.where(at_zh == e, block[8 * e:8 * e + 8], value)
            rows.append(value)
        ordered[16 * i:16 * i + 16, :] = jnp.concatenate(rows, axis=0).astype(BF16)
    place = weights_out.at[:, pl.ds(mine, half)]
    outs.append(local(ordered, place))
    last = remote(ordered, place, device(core=1 - core))

    for copy in outs:
        copy.wait()
    for copy in sent[-4:]:
        copy.wait_recv()
    for copy in sent:
        copy.wait_send()


def step_call(dims, old_order, new_order, step, grads, master, first, second):
    nx, ny, nzh, nzl, tiles, _ = dims
    nz, ns = nzh * nzl, nzh * nx
    half = tiles * LANES
    part = half // 2
    width = -(-tiles // nzl) * LANES
    blocks = ns * ny
    remotes = 2 + (ns - 1) + 2 * (nx - 1) + 2 * (ny - 1) + 2 * (nz - 1) + 2 * (ny - 1) + (nx - 1) + 4
    vmem = pltpu.VMEM
    f32_out = jax.ShapeDtypeStruct((ny // 2, 8, 2 * half), F32)
    anywhere = pl.BlockSpec(memory_space=pl.ANY)
    scalars = pl.BlockSpec(memory_space=pltpu.SMEM)
    return pl.pallas_call(
        functools.partial(kernel, dims),
        out_shape=(f32_out, f32_out, f32_out, jax.ShapeDtypeStruct((8 * blocks, 2 * half), BF16)),
        in_specs=[scalars] * 3 + [anywhere] * 4,
        out_specs=[anywhere] * 4,
        scratch_shapes=[
            vmem((2, 8 * blocks, part), BF16),
            vmem((2, 8 * blocks, part), BF16),
            vmem((2, blocks, 8, part), F32),
            vmem((3, ny, 8, width), F32),
            vmem((ns, 3, 8, width), F32),
            vmem((ns, 3, 8, width), F32),
            vmem((nx, ny, nzh, 8, part), F32),
            vmem((ny, nx, nzh, 8, part), F32),
            vmem((nx - 1, ny, nzh, 8, part), F32),
            vmem((ny - 1, nx, nzh, 8, part), F32),
            vmem((ny, nzh, 8, part), F32),
            vmem((nx, nzh, 8, part), F32),
            vmem((ny - 1, nzh, 8, part), F32),
            vmem((nx - 1, nzh, 8, part), F32),
            vmem((nzh, 8, half), F32),
            vmem((nz - 1, 8, width), F32),
            vmem((3, 8, width), F32),
            vmem((nzl, 3, 8, width), F32),
            vmem((max(nzh - 1, 1), nzl, 8, width), F32),
            vmem((3, 8, half), F32),
            vmem((ny, 3, 8, half), F32),
            vmem((nx, ny, 8 * nzh, half), BF16),
            vmem((8 * blocks, half), BF16),
            pltpu.SemaphoreType.DMA((remotes,)),
            pltpu.SemaphoreType.DMA((remotes,)),
            pltpu.SemaphoreType.DMA((16,)),
        ],
        compiler_params=pltpu.CompilerParams(
            collective_id=0, has_side_effects=True, vmem_limit_bytes=56 * 1024 * 1024
        ),
        cost_estimate=pl.CostEstimate(flops=4_000_000, bytes_accessed=8_000_000, transcendentals=0),
    )(old_order, new_order, step, grads, master, first, second)


def body(dims, master_old, moment_one_old, moment_two_old, grads, old_order, new_order, step):
    blocks, rows, columns = grads.shape[2:]
    flat = grads.reshape(blocks * rows, columns)
    master, first, second, weights = step_call(
        dims, old_order, new_order, step, flat, master_old, moment_one_old, moment_two_old
    )
    return master[None], first[None], second[None], weights.reshape(1, blocks, rows, columns)


def solution(mesh, dims=(4, 4, 2, 4, 18, 0)):
    return jax.shard_map(
        functools.partial(body, dims),
        mesh=mesh,
        in_specs=(
            P("shard", None, None),
            P("shard", None, None),
            P("shard", None, None),
            P("rep", "shard", None, None, None),
            P(),
            P(),
            P(),
        ),
        out_specs=(
            P("rep", "shard", None, None),
            P("rep", "shard", None, None),
            P("rep", "shard", None, None),
            P("rep", None, None, None),
        ),
        check_vma=False,
    )
```

time: 854 us -> 85.9 us (0.10)
  the two profiles are of different devices: /device:TPU:1 before, /device:TPU:33 now
where the time goes in v1:
time: 85.9 us; the launch traced here: 85.7 us
  Pallas kernels  76.1 us (89%)
  local copies, waits for them, and re-layouts  8.3 us (10%)
  between operations  1.29 us (2%)
    pallas_call x1, Pallas kernels, step_call(): pl.pallas_call(functools.partial(kernel, dims), out_shape=(f32_out, f32_o...  76.1 us
    unnamed x4, local copies, waits for them, and re-layouts  8.3 us

profile of v1, /device:TPU:33, one launch (start us, length us, event | category | flops | bytes accessed | tf_op | source)
XLA Modules:
  0.0 85.7 jit_solution(2381511447458976296)
XLA Ops:
  1.3 76.1 %shard_map.102 = (f32[2,8,4608]{2,1,0:T(8,128)}, f32[2,8,4608]{2,1,0:T(8,128)}, f32[2,8,4608]{2,1,0:T(8,128)}, bf16[256,4608]{1,0:T(8,128)(2,1)}) custom-call(s32[32]{0:T(128)} %old_ref.1, s32[32]{0:T(128)} %new_ref.1, s32[1]{0:T(128)S(6)} %copy.15.step_ref, bf16[256,4608]{1,0:T(8,128)(2,1)} %bitcast.5, f32[4,8,4608]{2,1,0:T(8,128)} %master.1, ...), custom_call_target="tpu_custom_call" | custom-call | flops 4000000 | bytes 8000000 | tf_op jit(solution)/shard_map/pallas_call | solution.py:326
  77.4 1.7 %copy.16 = f32[1,2,8,4608]{3,2,1,0:T(8,128)} copy(f32[1,2,8,4608]{3,2,1,0:T(8,128)} %bitcast.9) | data formatting | bytes 589824
  79.1 1.7 %copy.17 = f32[1,2,8,4608]{3,2,1,0:T(8,128)} copy(f32[1,2,8,4608]{3,2,1,0:T(8,128)} %bitcast.8) | data formatting | bytes 589824
  80.8 1.7 %copy.18 = f32[1,2,8,4608]{3,2,1,0:T(8,128)} copy(f32[1,2,8,4608]{3,2,1,0:T(8,128)} %bitcast.7) | data formatting | bytes 589824
  82.4 3.2 %copy.19 = bf16[1,32,8,4608]{3,2,1,0:T(8,128)(2,1)} copy(bf16[1,32,8,4608]{3,2,1,0:T(8,128)(2,1)} %bitcast.6) | data formatting | bytes 4718592

commit v2 on v0

v2 whole, which is shorter than its diff:
```python
import functools

import jax
import jax.numpy as jnp
import numpy as np
from jax import lax
from jax.experimental import pallas as pl
from jax.experimental.pallas import tpu as pltpu
from jax.sharding import PartitionSpec as P

MESH = pl.DeviceIdType.MESH
LANES = 128
F32 = jnp.float32
BF16 = jnp.bfloat16


def power(base, count):
    out = jnp.float32(1.0)
    for bit in range(11):
        factor = np.float32(float(base) ** (1 << bit))
        taken = lax.rem(lax.shift_right_logical(count, jnp.int32(bit)), jnp.int32(2)) == 1
        out = jnp.where(taken, out * factor, out)
    return jnp.where(count >= 2048, jnp.float32(0.0), out)


def kernel(
    dims, chunks, stop,
    old_ref, new_ref, step_ref, grads, master, first, second,
    gathered, pairs,
    state, state_out, cand, half_sum, recv3, result, result_z, short, short_z, wide, pair,
    send_sem, recv_sem, pair_sem, local_sem, *buffers,
):
    nx, ny, nzh, nzl, tiles = dims
    nz, ns, nb = nzh * nzl, nzh * nx, ny // 2
    half = tiles * LANES
    width = -(-tiles // nzl) * LANES
    fold = short.shape[1]
    starts = [(k * tiles // nzl) * LANES for k in range(nzl + 1)]

    rep, shard = lax.axis_index("rep"), lax.axis_index("shard")
    core = lax.rem(rep, 2)
    y = lax.rem(lax.div(rep, 2), ny)
    zl = lax.div(rep, 2 * ny)
    x, zh = lax.rem(shard, nx), lax.div(shard, nx)
    z = zh * nzl + zl

    def device(x=x, y=y, zh=zh, zl=zl, core=core):
        return ((zl * ny + y) * 2 + core, zh * nx + x)

    def ahead(value, by, size):
        return lax.rem(value + by, size)

    def piece(k):
        return pl.multiple_of(lax.div(k * tiles, nzl) * LANES, LANES)

    count = {"remote": 0, "local": 0}
    sent = []

    def remote(src, dst, to, sem=None):
        k = count["remote"]
        count["remote"] += 1
        copy = pltpu.make_async_remote_copy(
            src_ref=src, dst_ref=dst, send_sem=send_sem.at[k],
            recv_sem=recv_sem.at[k] if sem is None else sem,
            device_id=to, device_id_type=MESH,
        )
        copy.start()
        sent.append(copy)
        return copy

    def local(src, dst):
        k = count["local"]
        count["local"] += 1
        copy = pltpu.make_async_copy(src, dst, local_sem.at[k])
        copy.start()
        return copy

    def finish():
        for copy in sent:
            copy.wait_send()

    far = lambda n: sorted(range(1, n), key=lambda d: -min(d, n - d))

    parts, column = [], 0
    for k, (along_x, count_tiles) in enumerate(chunks):
        names = ("own", "sib", "chip", "send", "recv1", "part", "recv2")
        refs = dict(zip(names, buffers[len(names) * k:len(names) * (k + 1)]))
        refs.update(along_x=along_x, at=column, size=count_tiles * LANES)
        refs.update(n1=nx if along_x else ny, n2=ny if along_x else nx)
        refs.update(me1=x if along_x else y, me2=y if along_x else x)
        refs.update(axis1="x" if along_x else "y", axis2="y" if along_x else "x")
        parts.append(refs)
        column += count_tiles * LANES

    mine = pl.multiple_of(core * half, LANES)
    theirs = pl.multiple_of((1 - core) * half, LANES)
    for p in parts:
        p["load"] = local(grads.at[:, pl.ds(mine + p["at"], p["size"])], p["own"])
    spot = pl.ds(mine + piece(zl), width)
    state_loads = [local(ref.at[:, :, spot], state.at[k]) for k, ref in enumerate((master, first, second))]

    partners = [device(core=1 - core)]
    partners += [device(x=ahead(x, d, nx)) for d in range(1, nx)]
    for d in range(1, ny):
        partners += [device(y=ahead(y, d, ny)), device(y=ahead(y, d, ny), core=1 - core)]
    for d in range(1, nz):
        other = ahead(z, d, nz)
        partners.append(device(zh=lax.div(other, nzl), zl=lax.rem(other, nzl)))
    for e in range(1, nzh):
        partners += [device(x=ahead(x, d, nx), zh=ahead(zh, e, nzh)) for d in range(1, nx)]
    barrier = pltpu.get_barrier_semaphore()
    for partner in partners:
        pl.semaphore_signal(barrier, inc=1, device_id=partner, device_id_type=MESH)
    pl.semaphore_wait(barrier, len(partners))

    for p in parts:
        p["swap"] = remote(grads.at[:, pl.ds(theirs + p["at"], p["size"])], p["sib"], device(core=1 - core))

    for copy in state_loads:
        copy.wait()
    for e in range(nzh):
        for d in range(nx):
            wanted = new_ref[(ahead(zh, e, nzh) * nx + ahead(x, d, nx)) * ny + y]
            pick = jnp.int32(0)
            for j in range(1, ny):
                pick = jnp.where(old_ref[shard * ny + j] == wanted, jnp.int32(j), pick)
            slot = e * nx + d
            target = state_out if slot else cand
            for k in range(3):
                target[slot, k] = state[k, pick]

    for p in parts:
        p["load"].wait()
        p["swap"].wait_recv()

        def add(i, carry, p=p):
            rows = pl.ds(pl.multiple_of(i * 16, 16), 16)
            both = p["own"][rows, :].astype(F32) + p["sib"][rows, :].astype(F32)
            p["chip"][2 * i] = both[:8]
            p["chip"][2 * i + 1] = both[8:]
            return carry

        lax.fori_loop(0, ns * ny // 2, add, 0)
        p["first"] = {}
        for d in far(p["n1"]) + [0]:
            lead = ahead(p["me1"], d, p["n1"])
            for inner in range(p["n2"]):
                for e in range(nzh):
                    to_x, to_y = (lead, inner) if p["along_x"] else (inner, lead)
                    p["send"][lead, inner, e] = p["chip"][new_ref[(e * nx + to_x) * ny + to_y]]
            if d:
                p["first"][d] = remote(p["send"].at[lead], p["recv1"].at[d - 1], device(**{p["axis1"]: lead}))

    if stop == 2:
        for p in parts:
            for copy in p["first"].values():
                copy.wait_recv()
        return finish()

    moves = {}
    for e in range(nzh - 1, -1, -1):
        for d in far(nx) + [0]:
            slot = e * nx + d
            if slot:
                moves[slot] = remote(
                    state_out.at[slot], cand.at[slot], device(x=ahead(x, d, nx), zh=ahead(zh, e, nzh))
                )

    for p in parts:
        for d in far(p["n1"]):
            p["first"][d].wait_recv()
        p["second"] = {}
        for d in far(p["n2"]) + [0]:
            to = ahead(p["me2"], d, p["n2"])
            for e in range(nzh):
                total = p["send"][p["me1"], to, e]
                for q in range(p["n1"] - 1):
                    total = total + p["recv1"][q, to, e]
                p["part"][to, e] = total
            if d:
                p["second"][d] = remote(p["part"].at[to], p["recv2"].at[d - 1], device(**{p["axis2"]: to}))
    for p in parts:
        for d in far(p["n2"]):
            p["second"][d].wait_recv()
        for e in range(nzh):
            total = p["part"][p["me2"], e]
            for q in range(p["n2"] - 1):
                total = total + p["recv2"][q, e]
            half_sum[e, :, p["at"]:p["at"] + p["size"]] = total

    third = {}
    for d in far(nz):
        other = ahead(z, d, nz)
        to_zh, to_zl = lax.div(other, nzl), lax.rem(other, nzl)
        third[d] = remote(
            half_sum.at[to_zh, :, pl.ds(piece(to_zl), width)], recv3.at[d - 1], device(zh=to_zh, zl=to_zl)
        )

    wanted = new_ref[shard * ny + y]
    pick = jnp.int32(0)
    for e in range(nzh):
        for d in range(nx):
            slot = e * nx + d
            if slot:
                moves[slot].wait_recv()
                from_x, from_zh = ahead(x, nx - d, nx), ahead(zh, nzh - e, nzh)
                for j in range(ny):
                    match = old_ref[(from_zh * nx + from_x) * ny + j] == wanted
                    pick = jnp.where(match, jnp.int32(slot), pick)
    t = step_ref[0]
    fix_one = 1.0 - power(0.9, t)
    fix_two = 1.0 - power(0.95, t)

    if stop == 3:
        for d in range(1, nz):
            third[d].wait_recv()
        return finish()

    for d in far(nz):
        third[d].wait_recv()
    grad = half_sum[zh, :, pl.ds(piece(zl), width)]
    for q in range(nz - 1):
        grad = grad + recv3[q]
    weight = cand[pick, 0]
    moment_one = 0.9 * cand[pick, 1] + 0.1 * grad
    moment_two = 0.95 * cand[pick, 2] + 0.05 * grad * grad
    direction = moment_one / fix_one / (jnp.sqrt(moment_two / fix_two) + 1e-08)
    updated = weight - 0.1 * (direction + 0.1 * weight)

    rest = updated[:, fold:]
    if rest.shape[1] < fold:
        rest = jnp.concatenate([rest, jnp.zeros((8, fold - rest.shape[1]), F32)], axis=1)
    short[...] = jnp.concatenate([updated[:, :fold], rest], axis=0).astype(BF16)
    short_z[z] = short[...]
    over_z = {}
    for d in far(nz):
        other = ahead(z, d, nz)
        over_z[d] = remote(short, short_z.at[z], device(zh=lax.div(other, nzl), zl=lax.rem(other, nzl)))

    for k, value in enumerate((updated, moment_one, moment_two)):
        result[k] = value
        result_z[zl, k] = value
    over_zl = {}
    for d in far(nzl):
        to = ahead(zl, d, nzl)
        over_zl[d] = remote(result, result_z.at[zl], device(zl=to))

    for d in far(nz):
        over_z[d].wait_recv()
    for k in range(nzl):
        span = starts[k + 1] - starts[k]
        for low, high, top in ((0, min(span, fold), 0), (fold, span, 8)):
            if high > low:
                rows = [short_z[e * nzl + k, :, :high - low].astype(F32)[top:top + 8] for e in range(nzh)]
                wide[:, starts[k] + low:starts[k] + high] = jnp.concatenate(rows, axis=0).astype(BF16)
    place = gathered.at[x, y, :, pl.ds(mine, half)]
    over_y = {}
    for d in far(ny):
        over_y[d] = remote(wide, place, device(y=ahead(y, d, ny)))
    kept = local(wide, place)

    for d in far(nzl):
        over_zl[d].wait_recv()
    for k in range(nzl):
        for a in range(3):
            pair[a, :, starts[k]:starts[k + 1]] = result_z[k, a, :, :starts[k + 1] - starts[k]]
    member, row = lax.div(y, nb), lax.rem(y, nb)
    pair_place = pairs.at[:, row, :, pl.ds(mine, half)]
    pair_mark = pair_sem.at[row * 2 + core]
    for d in far(ny):
        remote(pair, pair_place, device(y=ahead(y, d, ny), core=member), pair_mark)
    across = pltpu.make_async_remote_copy(
        src_ref=pair, dst_ref=pair_place, send_sem=send_sem.at[count["remote"]], recv_sem=pair_mark,
        device_id=device(core=1 - core), device_id_type=MESH,
    )
    count["remote"] += 1
    within = pltpu.make_async_copy(pair, pair_place, pair_mark)

    @pl.when(member == core)
    def _():
        within.start()

    @pl.when(member != core)
    def _():
        across.start()

    for d in far(ny):
        over_y[d].wait_recv()
    kept.wait()
    place = gathered.at[x, :, :, pl.ds(mine, half)]
    over_x = {}
    for d in far(nx):
        over_x[d] = remote(place, place, device(x=ahead(x, d, nx)))
    given = [remote(place, place, device(core=1 - core))]
    for d in far(nx)[::-1]:
        over_x[d].wait_recv()
        place = gathered.at[ahead(x, nx - d, nx), :, :, pl.ds(mine, half)]
        given.append(remote(place, place, device(core=1 - core)))

    for r in range(nb):
        for c in range(2):
            pltpu.make_async_copy(pair, pairs.at[:, r, :, pl.ds(c * half, half)], pair_sem.at[r * 2 + c]).wait()

    @pl.when(member != core)
    def _():
        across.wait_send()

    for copy in given:
        copy.wait_recv()
    finish()


def spread_kernel(dims, new_ref, gathered, pairs, master_out, first_out, second_out, weights_out, sem):
    nx, ny, nzh, _, _ = dims
    copies = []
    for a, ref in enumerate((master_out, first_out, second_out)):
        copies.append(pltpu.make_async_copy(pairs.at[a], ref, sem.at[a]))
    for k in range(nzh * nx * ny):
        e, at_x, at_y = k // (nx * ny), k // ny % nx, k % ny
        copies.append(
            pltpu.make_async_copy(gathered.at[(at_x * ny + at_y) * nzh + e], weights_out.at[new_ref[k]], sem.at[3 + k])
        )
    for copy in copies:
        copy.start()
    for copy in copies:
        copy.wait()


def step_call(dims, chunks, stop, old_order, new_order, step, grads, master, first, second):
    nx, ny, nzh, nzl, tiles = dims
    nz, ns, nb = nzh * nzl, nzh * nx, ny // 2
    half = tiles * LANES
    width = -(-tiles // nzl) * LANES
    fold = -(-width // (2 * LANES)) * LANES
    blocks = ns * ny
    remotes = 80
    vmem = pltpu.VMEM
    anywhere = pl.BlockSpec(memory_space=pl.ANY)
    outside = pl.BlockSpec(memory_space=pltpu.HBM)
    scalars = pl.BlockSpec(memory_space=pltpu.SMEM)
    inside = pl.BlockSpec(memory_space=pltpu.VMEM)
    buffers = []
    for along_x, count_tiles in chunks:
        n1, n2 = (nx, ny) if along_x else (ny, nx)
        size = count_tiles * LANES
        buffers += [
            vmem((8 * blocks, size), BF16),
            vmem((8 * blocks, size), BF16),
            vmem((blocks, 8, size), F32),
            vmem((n1, n2, nzh, 8, size), F32),
            vmem((n1 - 1, n2, nzh, 8, size), F32),
            vmem((n2, nzh, 8, size), F32),
            vmem((n2 - 1, nzh, 8, size), F32),
        ]
    gathered, pairs = pl.pallas_call(
        functools.partial(kernel, dims, chunks, stop),
        out_shape=(pltpu.VMEM((nx, ny, 8 * nzh, 2 * half), BF16), pltpu.VMEM((3, nb, 8, 2 * half), F32)),
        in_specs=[scalars] * 3 + [outside] * 4,
        out_specs=[inside] * 2,
        scratch_shapes=[
            vmem((3, ny, 8, width), F32),
            vmem((ns, 3, 8, width), F32),
            vmem((ns, 3, 8, width), F32),
            vmem((nzh, 8, half), F32),
            vmem((nz - 1, 8, width), F32),
            vmem((3, 8, width), F32),
            vmem((nzl, 3, 8, width), F32),
            vmem((16, fold), BF16),
            vmem((nz, 16, fold), BF16),
            vmem((8 * nzh, half), BF16),
            vmem((3, 8, half), F32),
            pltpu.SemaphoreType.DMA((remotes,)),
            pltpu.SemaphoreType.DMA((remotes,)),
            pltpu.SemaphoreType.DMA((2 * nb,)),
            pltpu.SemaphoreType.DMA((16,)),
        ] + buffers,
        compiler_params=pltpu.CompilerParams(
            collective_id=0, has_side_effects=True, vmem_limit_bytes=60 * 1024 * 1024
        ),
        cost_estimate=pl.CostEstimate(flops=4_000_000, bytes_accessed=8_000_000, transcendentals=0),
    )(old_order, new_order, step, grads, master, first, second)
    f32_out = jax.ShapeDtypeStruct((nb, 8, 2 * half), F32)
    return pl.pallas_call(
        functools.partial(spread_kernel, dims),
        out_shape=(f32_out, f32_out, f32_out, jax.ShapeDtypeStruct((blocks, 8, 2 * half), BF16)),
        in_specs=[scalars, inside, inside],
        out_specs=[anywhere] * 4,
        scratch_shapes=[pltpu.SemaphoreType.DMA((3 + blocks,))],
        compiler_params=pltpu.CompilerParams(vmem_limit_bytes=8 * 1024 * 1024),
    )(new_order, gathered.reshape(blocks, 8, 2 * half), pairs)


def body(dims, chunks, stop, master_old, moment_one_old, moment_two_old, grads, old_order, new_order, step):
    blocks, rows, columns = grads.shape[2:]
    flat = grads.reshape(blocks * rows, columns)
    master, first, second, weights = step_call(
        dims, chunks, stop, old_order, new_order, step, flat, master_old, moment_one_old, moment_two_old
    )
    return master[None], first[None], second[None], weights[None]


CHUNKS = ((True, 5), (False, 5), (True, 4), (False, 4))


def solution(mesh, dims=(4, 4, 2, 4, 18), chunks=CHUNKS, stop=0):
    return jax.shard_map(
        functools.partial(body, dims, chunks, stop),
        mesh=mesh,
        in_specs=(
            P("shard", None, None),
            P("shard", None, None),
            P("shard", None, None),
            P("rep", "shard", None, None, None),
            P(),
            P(),
            P(),
        ),
        out_specs=(
            P("rep", "shard", None, None),
            P("rep", "shard", None, None),
            P("rep", "shard", None, None),
            P("rep", None, None, None),
        ),
        check_vma=False,
    )
```

time: 854 us -> 74.4 us (0.09)
  waiting for transfers between devices: 807 us -> 0 us
  Pallas kernels: 0 us -> 73 us
  local copies, waits for them, and re-layouts: 16.7 us -> 0.01 us
  between operations: 15 us -> 1.32 us
  other arithmetic: 12 us -> 0 us
    all_gather x4 -> x0, waiting for transfers between devices: 408 us -> none  [the longest x1 112 us: body(): lax.all_gather(moment_two_old, 'shard', axis=0, tiled=True)]
    psum x1 -> x0, waiting for transfers between devices: 260 us -> none  [body(): summed = lax.psum(ordered.astype(jnp.float32), 'rep')]
    reduce_scatter x1 -> x0, waiting for transfers between devices: 136 us -> none  [body(): lax.psum_scatter(summed, 'shard', scatter_dimension=0, tiled=True)]
    pallas_call x0 -> x2, Pallas kernels: none -> 73 us  [the longest x1 70.5 us: step_call(): pl.pallas_call(functools.partial(kernel, dims, chunks, stop), out_shape=(...]
    gather x6 -> x0, local copies, waits for them, and re-layouts: 15.2 us -> none  [the longest x1 3.77 us: body(): weights = jnp.take(gathered, new_slot_of, axis=0)]
  transfers between devices with their start and end apart: 7 -> 0, of which waited for: 7 -> 0; matrix products, arithmetic and copies ran while one was open for 1% -> 0% of each run, Pallas kernels for 0% -> 0%
where the time goes in v2:
time: 74.4 us; the launch traced here: 74.3 us
  Pallas kernels  73 us (98%)
  between operations  1.32 us (2%)
    pallas_call x1, Pallas kernels, step_call(): pl.pallas_call(functools.partial(kernel, dims, chunks, stop), out_shape=(...  70.5 us
    pallas_call x1, Pallas kernels, step_call(): pl.pallas_call(functools.partial(spread_kernel, dims), out_shape=(f32_out...  2.53 us

profile of v2, /device:TPU:1, one launch (start us, length us, event | category | flops | bytes accessed | tf_op | source)
XLA Modules:
  0.0 74.3 jit_solution(11736871750664901522)
XLA Ops:
  0.6 0.0 copy-start
  1.3 70.5 %shard_map.102 = (bf16[4,4,16,4608]{3,2,1,0:T(8,128)(2,1)S(1)}, f32[3,2,8,4608]{3,2,1,0:T(8,128)S(1)}) custom-call(s32[32]{0:T(128)} %old_ref.1, s32[32]{0:T(128)} %new_ref.3, s32[1]{0:T(128)S(6)} %copy.11.step_ref, bf16[256,4608]{1,0:T(8,128)(2,1)} %bitcast.7, f32[4,8,4608]{2,1,0:T(8,128)} %master.1, f32[4,8,4608]{2,1,0:T(8,128)} %first.1, f32[4,8,4608]{2,1,0:T(8,128)} %second.1), custom_call_target="tpu_custom_call" | custom-call | flops 4000000 | bytes 8000000 | tf_op jit(solution)/shard_map/pallas_call | solution.py:355
  71.8 0.0 copy-done
  71.8 2.5 %shard_map.103 = (f32[2,8,4608]{2,1,0:T(8,128)}, f32[2,8,4608]{2,1,0:T(8,128)}, f32[2,8,4608]{2,1,0:T(8,128)}, bf16[32,8,4608]{2,1,0:T(8,128)(2,1)}) custom-call(s32[32]{0:T(128)S(1)} %copy-done, bf16[32,8,4608]{2,1,0:T(8,128)(2,1)S(1)} %bitcast.6, f32[3,2,8,4608]{3,2,1,0:T(8,128)S(1)} %get-tuple-element.11.pairs), custom_call_target="tpu_custom_call" | custom-call | tf_op jit(solution)/shard_map/pallas_call | solution.py:383
Async XLA Ops:
  0.6 71.2 %copy-start = (s32[32]{0:T(128)S(1)}, s32[32]{0:T(128)}, u32[]{:S(2)}) copy-start(s32[32]{0:T(128)} %new_ref.3) | copy-start | bytes 388

commit v3 on v2

--- a/solution.py
+++ b/solution.py
@@ -27,8 +27,8 @@
     dims, chunks, stop,
     old_ref, new_ref, step_ref, grads, master, first, second,
     gathered, pairs,
-    state, state_out, cand, half_sum, recv3, result, result_z, short, short_z, wide, pair,
-    send_sem, recv_sem, pair_sem, local_sem, *buffers,
+    state, state_out, cand, turn, owned, half_sum, recv3, result, result_z, short, short_z, wide, pair,
+    send_sem, recv_sem, pair_sem, state_sem, local_sem, *buffers,
 ):
     nx, ny, nzh, nzl, tiles = dims
     nz, ns, nb = nzh * nzl, nzh * nx, ny // 2
@@ -54,7 +54,7 @@
         return pl.multiple_of(lax.div(k * tiles, nzl) * LANES, LANES)
 
     count = {"remote": 0, "local": 0}
-    sent = []
+    sent, moves, turns = [], [], []
 
     def remote(src, dst, to, sem=None):
         k = count["remote"]
@@ -78,12 +78,16 @@
     def finish():
         for copy in sent:
             copy.wait_send()
+        for copy in moves:
+            pl.when(holds)(copy.wait_send)
+        for q, copy in enumerate(turns):
+            pl.when(jnp.logical_and(holds, y != q))(copy.wait_send)
 
     far = lambda n: sorted(range(1, n), key=lambda d: -min(d, n - d))
 
     parts, column = [], 0
     for k, (along_x, count_tiles) in enumerate(chunks):
-        names = ("own", "sib", "chip", "send", "recv1", "part", "recv2")
+        names = ("own", "sib", "chip", "send", "relay", "recv1", "part", "recv2")
         refs = dict(zip(names, buffers[len(names) * k:len(names) * (k + 1)]))
         refs.update(along_x=along_x, at=column, size=count_tiles * LANES)
         refs.update(n1=nx if along_x else ny, n2=ny if along_x else nx)
@@ -118,22 +122,34 @@
 
     for copy in state_loads:
         copy.wait()
-    for e in range(nzh):
-        for d in range(nx):
-            wanted = new_ref[(ahead(zh, e, nzh) * nx + ahead(x, d, nx)) * ny + y]
+    holds = y < 3
+    kind = jnp.where(holds, y, 2)
+    for e in range(nzh - 1, -1, -1):
+        for d in far(nx) + [0]:
+            to_x, to_zh = ahead(x, d, nx), ahead(zh, e, nzh)
+            to_slot = (to_zh * nx + to_x) * ny
             pick = jnp.int32(0)
             for j in range(1, ny):
-                pick = jnp.where(old_ref[shard * ny + j] == wanted, jnp.int32(j), pick)
+                block = old_ref[shard * ny + j]
+                for q in range(ny):
+                    pick = jnp.where(new_ref[to_slot + q] == block, jnp.int32(j), pick)
             slot = e * nx + d
             target = state_out if slot else cand
-            for k in range(3):
-                target[slot, k] = state[k, pick]
-
-    for p in parts:
+            target[slot] = state[kind, pick]
+            if slot:
+                copy = pltpu.make_async_remote_copy(
+                    src_ref=state_out.at[slot], dst_ref=cand.at[slot],
+                    send_sem=state_sem.at[0, slot], recv_sem=state_sem.at[1, slot],
+                    device_id=device(x=to_x, zh=to_zh), device_id_type=MESH,
+                )
+                moves.append(copy)
+                pl.when(holds)(copy.start)
+
+    def chip_sum(p):
         p["load"].wait()
         p["swap"].wait_recv()
 
-        def add(i, carry, p=p):
+        def add(i, carry):
             rows = pl.ds(pl.multiple_of(i * 16, 16), 16)
             both = p["own"][rows, :].astype(F32) + p["sib"][rows, :].astype(F32)
             p["chip"][2 * i] = both[:8]
@@ -141,40 +157,102 @@
             return carry
 
         lax.fori_loop(0, ns * ny // 2, add, 0)
-        p["first"] = {}
-        for d in far(p["n1"]) + [0]:
-            lead = ahead(p["me1"], d, p["n1"])
-            for inner in range(p["n2"]):
-                for e in range(nzh):
-                    to_x, to_y = (lead, inner) if p["along_x"] else (inner, lead)
-                    p["send"][lead, inner, e] = p["chip"][new_ref[(e * nx + to_x) * ny + to_y]]
-            if d:
-                p["first"][d] = remote(p["send"].at[lead], p["recv1"].at[d - 1], device(**{p["axis1"]: lead}))
+
+    def order(p, lead):
+        for inner in range(p["n2"]):
+            for e in range(nzh):
+                to_x, to_y = (lead, inner) if p["along_x"] else (inner, lead)
+                p["send"][lead, inner, e] = p["chip"][new_ref[(e * nx + to_x) * ny + to_y]]
+
+    def first_step(p):
+        chip_sum(p)
+        n, me, h = p["n1"], p["me1"], p["n2"] // 2
+        low, high = pl.ds(0, h), pl.ds(h, h)
+        up, down = ahead(me, 1, n), ahead(me, n - 1, n)
+        if n == 2:
+            order(p, up)
+            p["got"] = [remote(p["send"].at[up], p["recv1"].at[0], device(**{p["axis1"]: up}))]
+            order(p, me)
+            return
+        to_up, to_down = device(**{p["axis1"]: up}), device(**{p["axis1"]: down})
+        across = ahead(me, 2, n)
+        order(p, across)
+        p["relays"] = [
+            remote(p["send"].at[across, low], p["relay"].at[0], to_up),
+            remote(p["send"].at[across, high], p["relay"].at[1], to_down),
+        ]
+        order(p, up)
+        p["got"] = [remote(p["send"].at[up, high], p["recv1"].at[0, high], to_up)]
+        order(p, down)
+        p["got"].append(remote(p["send"].at[down, low], p["recv1"].at[1, low], to_down))
+        order(p, me)
+
+    def second_step(p):
+        n, me, h = p["n1"], p["me1"], p["n2"] // 2
+        if n == 2:
+            return
+        low, high = pl.ds(0, h), pl.ds(h, h)
+        up, down = ahead(me, 1, n), ahead(me, n - 1, n)
+        to_up, to_down = device(**{p["axis1"]: up}), device(**{p["axis1"]: down})
+        p["relays"][0].wait_recv()
+        p["send"][up, low] = p["send"][up, low] + p["relay"][0]
+        p["got"].append(remote(p["send"].at[up, low], p["recv1"].at[0, low], to_up))
+        p["relays"][1].wait_recv()
+        p["send"][down, high] = p["send"][down, high] + p["relay"][1]
+        p["got"].append(remote(p["send"].at[down, high], p["recv1"].at[1, high], to_down))
+
+    for k, p in enumerate(parts):
+        first_step(p)
+        if k >= 2:
+            second_step(parts[k - 2])
+    for p in parts[-2:]:
+        second_step(p)
 
     if stop == 2:
         for p in parts:
-            for copy in p["first"].values():
+            for copy in p["got"]:
                 copy.wait_recv()
+        for copy in moves:
+            pl.when(holds)(copy.wait_recv)
         return finish()
 
-    moves = {}
-    for e in range(nzh - 1, -1, -1):
-        for d in far(nx) + [0]:
-            slot = e * nx + d
-            if slot:
-                moves[slot] = remote(
-                    state_out.at[slot], cand.at[slot], device(x=ahead(x, d, nx), zh=ahead(zh, e, nzh))
-                )
+    picks = []
+    for q in range(ny):
+        wanted = new_ref[shard * ny + q]
+        pick = jnp.int32(0)
+        for e in range(nzh):
+            for d in range(nx):
+                if e or d:
+                    from_x, from_zh = ahead(x, nx - d, nx), ahead(zh, nzh - e, nzh)
+                    for j in range(ny):
+                        match = old_ref[(from_zh * nx + from_x) * ny + j] == wanted
+                        pick = jnp.where(match, jnp.int32(e * nx + d), pick)
+        picks.append(pick)
+    for copy in moves:
+        pl.when(holds)(copy.wait_recv)
+    for q in range(ny):
+        turn[q] = cand[picks[q]]
+        copy = pltpu.make_async_remote_copy(
+            src_ref=turn.at[q], dst_ref=owned.at[kind],
+            send_sem=state_sem.at[2, q], recv_sem=state_sem.at[3, kind],
+            device_id=device(y=q), device_id_type=MESH,
+        )
+        turns.append(copy)
+        pl.when(jnp.logical_and(holds, y != q))(copy.start)
+
+    @pl.when(holds)
+    def _():
+        owned[kind] = turn[y]
 
     for p in parts:
-        for d in far(p["n1"]):
-            p["first"][d].wait_recv()
+        for copy in p["got"]:
+            copy.wait_recv()
         p["second"] = {}
         for d in far(p["n2"]) + [0]:
             to = ahead(p["me2"], d, p["n2"])
             for e in range(nzh):
                 total = p["send"][p["me1"], to, e]
-                for q in range(p["n1"] - 1):
+                for q in range(min(p["n1"] - 1, 2)):
                     total = total + p["recv1"][q, to, e]
                 p["part"][to, e] = total
             if d:
@@ -196,17 +274,9 @@
             half_sum.at[to_zh, :, pl.ds(piece(to_zl), width)], recv3.at[d - 1], device(zh=to_zh, zl=to_zl)
         )
 
-    wanted = new_ref[shard * ny + y]
-    pick = jnp.int32(0)
-    for e in range(nzh):
-        for d in range(nx):
-            slot = e * nx + d
-            if slot:
-                moves[slot].wait_recv()
-                from_x, from_zh = ahead(x, nx - d, nx), ahead(zh, nzh - e, nzh)
-                for j in range(ny):
-                    match = old_ref[(from_zh * nx + from_x) * ny + j] == wanted
-                    pick = jnp.where(match, jnp.int32(slot), pick)
+    for k in range(3):
+        copy = pltpu.make_async_copy(owned.at[k], owned.at[k], state_sem.at[3, k])
+        pl.when(y != k)(copy.wait)
     t = step_ref[0]
     fix_one = 1.0 - power(0.9, t)
     fix_two = 1.0 - power(0.95, t)
@@ -221,9 +291,9 @@
     grad = half_sum[zh, :, pl.ds(piece(zl), width)]
     for q in range(nz - 1):
         grad = grad + recv3[q]
-    weight = cand[pick, 0]
-    moment_one = 0.9 * cand[pick, 1] + 0.1 * grad
-    moment_two = 0.95 * cand[pick, 2] + 0.05 * grad * grad
+    weight = owned[0]
+    moment_one = 0.9 * owned[1] + 0.1 * grad
+    moment_two = 0.95 * owned[2] + 0.05 * grad * grad
     direction = moment_one / fix_one / (jnp.sqrt(moment_two / fix_two) + 1e-08)
     updated = weight - 0.1 * (direction + 0.1 * weight)
 
@@ -288,14 +358,42 @@
         over_y[d].wait_recv()
     kept.wait()
     place = gathered.at[x, :, :, pl.ds(mine, half)]
-    over_x = {}
-    for d in far(nx):
-        over_x[d] = remote(place, place, device(x=ahead(x, d, nx)))
-    given = [remote(place, place, device(core=1 - core))]
-    for d in far(nx)[::-1]:
-        over_x[d].wait_recv()
-        place = gathered.at[ahead(x, nx - d, nx), :, :, pl.ds(mine, half)]
-        given.append(remote(place, place, device(core=1 - core)))
+    n, h = nx, ny // 2
+    low, high = pl.ds(0, h), pl.ds(h, h)
+    up, down = ahead(x, 1, n), ahead(x, n - 1, n)
+
+    def quarter(of, rows):
+        return gathered.at[of, rows, :, pl.ds(mine, half)]
+
+    def pass_on(of, rows, to):
+        return remote(quarter(of, rows), quarter(of, rows), to)
+
+    sibling = device(core=1 - core)
+    if n == 2:
+        comes = [pass_on(x, pl.ds(0, ny), device(x=up))]
+        given = [pass_on(x, pl.ds(0, ny), sibling)]
+        comes[0].wait_recv()
+        given.append(pass_on(up, pl.ds(0, ny), sibling))
+    else:
+        to_up, to_down = device(x=up), device(x=down)
+        from_down, from_up = [pass_on(x, low, to_up)], [pass_on(x, high, to_down)]
+        from_down.append(pass_on(x, high, to_up))
+        from_up.append(pass_on(x, low, to_down))
+        given = [pass_on(x, pl.ds(0, ny), sibling)]
+        from_down[0].wait_recv()
+        far_low = pass_on(down, low, to_up)
+        from_up[0].wait_recv()
+        far_high = pass_on(up, high, to_down)
+        given += [pass_on(down, low, sibling), pass_on(up, high, sibling)]
+        from_down[1].wait_recv()
+        given.append(pass_on(down, high, sibling))
+        from_up[1].wait_recv()
+        given.append(pass_on(up, low, sibling))
+        across_x = ahead(x, 2, n)
+        far_low.wait_recv()
+        given.append(pass_on(across_x, low, sibling))
+        far_high.wait_recv()
+        given.append(pass_on(across_x, high, sibling))
 
     for r in range(nb):
         for c in range(2):
@@ -348,7 +446,8 @@
             vmem((8 * blocks, size), BF16),
             vmem((blocks, 8, size), F32),
             vmem((n1, n2, nzh, 8, size), F32),
-            vmem((n1 - 1, n2, nzh, 8, size), F32),
+            vmem((2, n2 // 2, nzh, 8, size), F32),
+            vmem((min(n1 - 1, 2), n2, nzh, 8, size), F32),
             vmem((n2, nzh, 8, size), F32),
             vmem((n2 - 1, nzh, 8, size), F32),
         ]
@@ -359,8 +458,10 @@
         out_specs=[inside] * 2,
         scratch_shapes=[
             vmem((3, ny, 8, width), F32),
-            vmem((ns, 3, 8, width), F32),
-            vmem((ns, 3, 8, width), F32),
+            vmem((ns, 8, width), F32),
+            vmem((ns, 8, width), F32),
+            vmem((ny, 8, width), F32),
+            vmem((3, 8, width), F32),
             vmem((nzh, 8, half), F32),
             vmem((nz - 1, 8, width), F32),
             vmem((3, 8, width), F32),
@@ -372,6 +473,7 @@
             pltpu.SemaphoreType.DMA((remotes,)),
             pltpu.SemaphoreType.DMA((remotes,)),
             pltpu.SemaphoreType.DMA((2 * nb,)),
+            pltpu.SemaphoreType.DMA((4, ns)),
             pltpu.SemaphoreType.DMA((16,)),
         ] + buffers,
         compiler_params=pltpu.CompilerParams(

time: 74.4 us -> 68.9 us (0.926)
  Pallas kernels: 73 us -> 67.4 us
    pallas_call x1, Pallas kernels: 70.5 us -> 64.9 us  [step_call(): pl.pallas_call(functools.partial(kernel, dims, chunks, stop), out_shape=(...]
where the time goes in v3:
time: 68.9 us; the launch traced here: 68.8 us
  Pallas kernels  67.4 us (98%)
  between operations  1.32 us (2%)
    pallas_call x1, Pallas kernels, step_call(): pl.pallas_call(functools.partial(kernel, dims, chunks, stop), out_shape=(...  64.9 us
    pallas_call x1, Pallas kernels, step_call(): pl.pallas_call(functools.partial(spread_kernel, dims), out_shape=(f32_out...  2.53 us

profile of v3, /device:TPU:1, one launch (start us, length us, event | category | flops | bytes accessed | tf_op | source)
XLA Modules:
  0.0 68.8 jit_solution(8024671106171312433)
XLA Ops:
  0.6 0.0 copy-start
  1.3 64.9 %shard_map.102 = (bf16[4,4,16,4608]{3,2,1,0:T(8,128)(2,1)S(1)}, f32[3,2,8,4608]{3,2,1,0:T(8,128)S(1)}) custom-call(s32[32]{0:T(128)} %old_ref.1, s32[32]{0:T(128)} %new_ref.3, s32[1]{0:T(128)S(6)} %copy.11.step_ref, bf16[256,4608]{1,0:T(8,128)(2,1)} %bitcast.7, f32[4,8,4608]{2,1,0:T(8,128)} %master.1, f32[4,8,4608]{2,1,0:T(8,128)} %first.1, f32[4,8,4608]{2,1,0:T(8,128)} %second.1), custom_call_target="tpu_custom_call" | custom-call | flops 4000000 | bytes 8000000 | tf_op jit(solution)/shard_map/pallas_call | solution.py:454
  66.2 0.0 copy-done
  66.2 2.5 %shard_map.103 = (f32[2,8,4608]{2,1,0:T(8,128)}, f32[2,8,4608]{2,1,0:T(8,128)}, f32[2,8,4608]{2,1,0:T(8,128)}, bf16[32,8,4608]{2,1,0:T(8,128)(2,1)}) custom-call(s32[32]{0:T(128)S(1)} %copy-done, bf16[32,8,4608]{2,1,0:T(8,128)(2,1)S(1)} %bitcast.6, f32[3,2,8,4608]{3,2,1,0:T(8,128)S(1)} %get-tuple-element.11.pairs), custom_call_target="tpu_custom_call" | custom-call | tf_op jit(solution)/shard_map/pallas_call | solution.py:485
Async XLA Ops:
  0.6 65.6 %copy-start = (s32[32]{0:T(128)S(1)}, s32[32]{0:T(128)}, u32[]{:S(2)}) copy-start(s32[32]{0:T(128)} %new_ref.3) | copy-start | bytes 388

commit v4 on v0

v4 whole, which is shorter than its diff:
```python
import functools
from types import SimpleNamespace

import jax
import jax.numpy as jnp
import numpy as np
from jax import lax
from jax.experimental import pallas as pl
from jax.experimental.pallas import tpu as pltpu
from jax.sharding import PartitionSpec as P

MESH = pl.DeviceIdType.MESH
LANES = 128
MARKS = 91
F32 = jnp.float32
BF16 = jnp.bfloat16


def power(base, count):
    out = jnp.float32(1.0)
    for bit in range(11):
        factor = np.float32(float(base) ** (1 << bit))
        taken = lax.rem(lax.shift_right_logical(count, jnp.int32(bit)), jnp.int32(2)) == 1
        out = jnp.where(taken, out * factor, out)
    return jnp.where(count >= 2048, jnp.float32(0.0), out)


def kernel(
    dims, groups, stop,
    old_in, new_in, step_in, grads, master, first, second,
    gathered, pairs,
    old_ref, new_ref, step_ref,
    state, state_out, cand, turn, owned,
    sems, *buffers,
):
    nx, ny, nzh, nzl, tiles = dims
    nz, ns, nb = nzh * nzl, nzh * nx, ny // 2
    half = tiles * LANES

    rep, shard = lax.axis_index("rep"), lax.axis_index("shard")
    core = lax.rem(rep, 2)
    y = lax.rem(lax.div(rep, 2), ny)
    zl = lax.div(rep, 2 * ny)
    x, zh = lax.rem(shard, nx), lax.div(shard, nx)
    z = zh * nzl + zl

    def device(x=x, y=y, zh=zh, zl=zl, core=core):
        return ((zl * ny + y) * 2 + core, zh * nx + x)

    def on_x(to):
        return device(x=to)

    def on_y(to):
        return device(y=to)

    def ahead(value, by, size):
        return lax.rem(value + by, size)

    used = []
    ends = []

    def mark():
        used.append(1)
        return sems.at[len(used) - 1]

    def take(ref, sem):
        pltpu.make_async_copy(ref, ref, sem).wait()

    def remote(src, dst, to, send, recv, when=None):
        copy = pltpu.make_async_remote_copy(
            src_ref=src, dst_ref=dst, send_sem=send, recv_sem=recv, device_id=to, device_id_type=MESH
        )
        if when is None:
            copy.start()
        else:
            pl.when(when)(copy.start)

    def local(src, dst, sem):
        copy = pltpu.make_async_copy(src, dst, sem)
        copy.start()
        return copy

    def sends(ref, when=None):
        sem = mark()
        ends.append((ref, sem, when))
        return sem

    def finish():
        for ref, sem, when in ends:
            if when is None:
                take(ref, sem)
            else:
                pl.when(when)(functools.partial(take, ref, sem))

    far = lambda n: sorted(range(1, n), key=lambda d: -min(d, n - d))
    mine = pl.multiple_of(core * half, LANES)
    theirs = pl.multiple_of((1 - core) * half, LANES)
    sibling = device(core=1 - core)

    teams, column, k = [], 0, 0
    for chunks in groups:
        g = SimpleNamespace(at=column, parts=[], tiles=sum(n for _, n in chunks))
        inner = 0
        for along_x, count_tiles in chunks:
            p = SimpleNamespace(along_x=along_x, at=column + inner, inner=inner, size=count_tiles * LANES)
            p.own, p.sib, p.chip, p.send, p.relay, p.recv1, p.part, p.recv2 = buffers[k:k + 8]
            k += 8
            p.n1, p.n2, p.me1, p.me2 = (nx, ny, x, y) if along_x else (ny, nx, y, x)
            p.to1, p.to2 = (on_x, on_y) if along_x else (on_y, on_x)
            inner += count_tiles * LANES
            g.parts.append(p)
        g.sum, g.recv3, g.result, g.result_z, g.short, g.short_z, g.wide, g.pair = buffers[k:k + 8]
        k += 8
        g.size = inner
        g.width = g.result.shape[2]
        g.fold = g.short.shape[1]
        g.starts = [(q * g.tiles // nzl) * LANES for q in range(nzl + 1)]
        column += inner
        teams.append(g)

    def piece(g, q):
        return pl.multiple_of(lax.div(q * g.tiles, nzl) * LANES, LANES)

    small = [local(src, dst, mark()) for src, dst in ((old_in, old_ref), (new_in, new_ref), (step_in, step_ref))]
    for g in teams:
        for p in g.parts:
            p.load = local(grads.at[:, pl.ds(mine + p.at, p.size)], p.own, mark())
    state_mark, column = mark(), 0
    for g in teams:
        g.state_at = column
        for a, ref in enumerate((master, first, second)):
            spot = pl.ds(mine + g.at + piece(g, zl), g.width)
            local(ref.at[:, :, spot], state.at[a, :, :, pl.ds(column, g.width)], state_mark)
        column += g.width

    partners = [sibling]
    partners += [device(x=ahead(x, d, nx)) for d in range(1, nx)]
    for d in range(1, ny):
        partners += [device(y=ahead(y, d, ny)), device(y=ahead(y, d, ny), core=1 - core)]
    for d in range(1, nz):
        other = ahead(z, d, nz)
        partners.append(device(zh=lax.div(other, nzl), zl=lax.rem(other, nzl)))
    for e in range(1, nzh):
        partners += [device(x=ahead(x, d, nx), zh=ahead(zh, e, nzh)) for d in range(1, nx)]
    barrier = pltpu.get_barrier_semaphore()
    for partner in partners:
        pl.semaphore_signal(barrier, inc=1, device_id=partner, device_id_type=MESH)
    pl.semaphore_wait(barrier, len(partners))

    swap_send = sends(grads.at[:, pl.ds(0, half)])
    for g in teams:
        for p in g.parts:
            p.swap = mark()
            remote(grads.at[:, pl.ds(theirs + p.at, p.size)], p.sib, sibling, swap_send, p.swap)

    holds = y < 3
    kind = jnp.where(holds, y, 2)
    moved = state_out.at[pl.ds(1, ns - 1)]
    move_send, move_recv = sends(moved, holds), mark()
    turn_marks = [mark() for _ in range(3)]
    turn_send = mark()
    turn_recv = sems.at[kind + (len(used) - 4)]
    ends.append((turn.at[pl.ds(0, ny - 1)], turn_send, holds))

    def state_first():
        take(state, state_mark)
        for e in range(nzh - 1, -1, -1):
            for d in far(nx) + [0]:
                to_x, to_zh = ahead(x, d, nx), ahead(zh, e, nzh)
                to_slot = (to_zh * nx + to_x) * ny
                pick = jnp.int32(0)
                for j in range(1, ny):
                    block = old_ref[shard * ny + j]
                    for q in range(ny):
                        pick = jnp.where(new_ref[to_slot + q] == block, jnp.int32(j), pick)
                slot = e * nx + d
                target = state_out if slot else cand
                target[slot] = state[kind, pick]
                if slot:
                    to = device(x=to_x, zh=to_zh)
                    remote(state_out.at[slot], cand.at[slot], to, move_send, move_recv, holds)

    def state_second():
        picks = []
        for q in range(ny):
            wanted = new_ref[shard * ny + q]
            pick = jnp.int32(0)
            for e in range(nzh):
                for d in range(nx):
                    if e or d:
                        from_x, from_zh = ahead(x, nx - d, nx), ahead(zh, nzh - e, nzh)
                        for j in range(ny):
                            match = old_ref[(from_zh * nx + from_x) * ny + j] == wanted
                            pick = jnp.where(match, jnp.int32(e * nx + d), pick)
            picks.append(pick)
        pl.when(holds)(functools.partial(take, moved, move_recv))
        for q in range(ny):
            turn[q] = cand[picks[q]]
            away = jnp.logical_and(holds, y != q)
            remote(turn.at[q], owned.at[kind], device(y=q), turn_send, turn_recv, away)

        @pl.when(holds)
        def _():
            owned[kind] = turn[y]

    def state_done():
        for a in range(3):
            pl.when(y != a)(functools.partial(take, owned.at[a], turn_marks[a]))

    def chip_sum(p):
        p.load.wait()
        take(p.sib, p.swap)

        def add(i, carry):
            rows = pl.ds(pl.multiple_of(i * 16, 16), 16)
            both = p.own[rows, :].astype(F32) + p.sib[rows, :].astype(F32)
            p.chip[2 * i] = both[:8]
            p.chip[2 * i + 1] = both[8:]
            return carry

        lax.fori_loop(0, ns * ny // 2, add, 0)

    def order(p, lead):
        for inner in range(p.n2):
            for e in range(nzh):
                to_x, to_y = (lead, inner) if p.along_x else (inner, lead)
                p.send[lead, inner, e] = p.chip[new_ref[(e * nx + to_x) * ny + to_y]]

    def first_step(p):
        chip_sum(p)
        n, me, h = p.n1, p.me1, p.n2 // 2
        low, high = pl.ds(0, h), pl.ds(h, h)
        up, down = ahead(me, 1, n), ahead(me, n - 1, n)
        if n == 2:
            order(p, up)
            p.got = mark()
            remote(p.send.at[up], p.recv1.at[0], p.to1(up), sends(p.send.at[0]), p.got)
            order(p, me)
            return
        to_up, to_down = p.to1(up), p.to1(down)
        across = ahead(me, 2, n)
        order(p, across)
        p.relays, p.got, p.out = [mark(), mark()], mark(), sends(p.send.at[pl.ds(0, 3)])
        out, got = p.out, p.got
        remote(p.send.at[across, low], p.relay.at[0], to_up, out, p.relays[0])
        remote(p.send.at[across, high], p.relay.at[1], to_down, out, p.relays[1])
        order(p, up)
        remote(p.send.at[up, high], p.recv1.at[0, high], to_up, out, got)
        order(p, down)
        remote(p.send.at[down, low], p.recv1.at[1, low], to_down, out, got)
        order(p, me)

    def second_step(p):
        n, me, h = p.n1, p.me1, p.n2 // 2
        if n == 2:
            return
        low, high = pl.ds(0, h), pl.ds(h, h)
        up, down = ahead(me, 1, n), ahead(me, n - 1, n)
        to_up, to_down = p.to1(up), p.to1(down)
        take(p.relay.at[0], p.relays[0])
        p.send[up, low] = p.send[up, low] + p.relay[0]
        remote(p.send.at[up, low], p.recv1.at[0, low], to_up, p.out, p.got)
        take(p.relay.at[1], p.relays[1])
        p.send[down, high] = p.send[down, high] + p.relay[1]
        remote(p.send.at[down, high], p.recv1.at[1, high], to_down, p.out, p.got)

    def third_step(p):
        take(p.recv1, p.got)
        p.second, out = mark(), sends(p.recv2)
        for d in far(p.n2) + [0]:
            to = ahead(p.me2, d, p.n2)
            for e in range(nzh):
                total = p.send[p.me1, to, e]
                for q in range(min(p.n1 - 1, 2)):
                    total = total + p.recv1[q, to, e]
                p.part[to, e] = total
            if d:
                remote(p.part.at[to], p.recv2.at[d - 1], p.to2(to), out, p.second)

    def sum_z(g):
        for p in g.parts:
            take(p.recv2, p.second)
            for e in range(nzh):
                total = p.part[p.me2, e]
                for q in range(p.n2 - 1):
                    total = total + p.recv2[q, e]
                g.sum[e, :, p.inner:p.inner + p.size] = total
        g.third, out = mark(), sends(g.recv3)
        for d in far(nz):
            other = ahead(z, d, nz)
            to_zh, to_zl = lax.div(other, nzl), lax.rem(other, nzl)
            src = g.sum.at[to_zh, :, pl.ds(piece(g, to_zl), g.width)]
            remote(src, g.recv3.at[d - 1], device(zh=to_zh, zl=to_zl), out, g.third)

    def update(g, fix_one, fix_two):
        take(g.recv3, g.third)
        grad = g.sum[zh, :, pl.ds(piece(g, zl), g.width)]
        for q in range(nz - 1):
            grad = grad + g.recv3[q]
        spot = slice(g.state_at, g.state_at + g.width)
        weight = owned[0, :, spot]
        moment_one = 0.9 * owned[1, :, spot] + 0.1 * grad
        moment_two = 0.95 * owned[2, :, spot] + 0.05 * grad * grad
        direction = moment_one / fix_one / (jnp.sqrt(moment_two / fix_two) + 1e-08)
        updated = weight - 0.1 * (direction + 0.1 * weight)
        fold, short, short_z = g.fold, g.short, g.short_z
        rest = updated[:, fold:]
        if rest.shape[1] < fold:
            rest = jnp.concatenate([rest, jnp.zeros((8, fold - rest.shape[1]), F32)], axis=1)
        short[...] = jnp.concatenate([updated[:, :fold], rest], axis=0).astype(BF16)
        g.over_z, out = mark(), sends(short_z.at[pl.ds(0, nz - 1)])
        for d in far(nz):
            other = ahead(z, d, nz)
            to = device(zh=lax.div(other, nzl), zl=lax.rem(other, nzl))
            remote(short, short_z.at[z], to, out, g.over_z)
        short_z[z] = short[...]
        for a, value in enumerate((updated, moment_one, moment_two)):
            g.result[a] = value
            g.result_z[zl, a] = value

    def block_place(g, of_x, of_y):
        return gathered.at[of_x, of_y, :, pl.ds(mine + g.at, g.size)]

    def weights_y(g):
        take(g.short_z.at[pl.ds(0, nz - 1)], g.over_z)
        starts, fold = g.starts, g.fold
        for q in range(nzl):
            span = starts[q + 1] - starts[q]
            for low, high, top in ((0, min(span, fold), 0), (fold, span, 8)):
                if high > low:
                    rows = [g.short_z[e * nzl + q, :, :high - low].astype(F32)[top:top + 8] for e in range(nzh)]
                    g.wide[:, starts[q] + low:starts[q] + high] = jnp.concatenate(rows, axis=0).astype(BF16)
        place = block_place(g, x, y)
        rest = gathered.at[0, pl.ds(0, ny - 1), :, pl.ds(0, g.size)]
        g.over_y, out = mark(), sends(rest)
        for d in far(ny):
            remote(g.wide, place, device(y=ahead(y, d, ny)), out, g.over_y)
        g.kept = local(g.wide, place, mark())

    def masters_z(g):
        if nzl > 1:
            g.over_zl, out = mark(), sends(g.result_z.at[pl.ds(0, nzl - 1)])
        for d in far(nzl):
            remote(g.result, g.result_z.at[zl], device(zl=ahead(zl, d, nzl)), out, g.over_zl)

    member, row = lax.div(y, nb), lax.rem(y, nb)

    def pairs_y(g):
        if nzl > 1:
            take(g.result_z.at[pl.ds(0, nzl - 1)], g.over_zl)
        starts = g.starts
        for q in range(nzl):
            for a in range(3):
                g.pair[a, :, starts[q]:starts[q + 1]] = g.result_z[q, a, :, :starts[q + 1] - starts[q]]
        place = pairs.at[:, row, :, pl.ds(mine + g.at, g.size)]
        first_mark = len(used)
        g.pair_marks = [mark() for _ in range(2 * nb)]
        landed = sems.at[first_mark + row * 2 + core]
        for d in far(ny):
            remote(g.pair, place, device(y=ahead(y, d, ny), core=member), sends(g.pair), landed)
        remote(g.pair, place, sibling, sends(g.pair, member != core), landed, member != core)
        within = pltpu.make_async_copy(g.pair, place, landed)
        pl.when(member == core)(within.start)

    def pairs_done(g):
        for k in range(2 * nb):
            take(g.pair, g.pair_marks[k])

    h = ny // 2
    low, high = pl.ds(0, h), pl.ds(h, h)
    up, down = ahead(x, 1, nx), ahead(x, nx - 1, nx)

    def pass_on(g, of, rows, to, send, recv):
        place = gathered.at[of, rows, :, pl.ds(mine + g.at, g.size)]
        remote(place, place, to, send, recv)

    def span(g, of, rows):
        return gathered.at[of, rows, :, pl.ds(0, g.size)]

    every = pl.ds(0, ny)

    def weights_x(g):
        take(span(g, 0, pl.ds(0, ny - 1)), g.over_y)
        g.kept.wait()
        g.given, g.give = mark(), sends(span(g, pl.ds(0, nx), every))
        if nx == 2:
            g.near = mark()
            pass_on(g, x, every, device(x=up), sends(span(g, 0, every)), g.near)
            pass_on(g, x, every, sibling, g.give, g.given)
            return
        to_up, to_down = device(x=up), device(x=down)
        g.out = sends(span(g, pl.ds(0, 3), every))
        g.come = [mark(), mark()]
        g.near = mark()
        pass_on(g, x, low, to_up, g.out, g.come[0])
        pass_on(g, x, high, to_down, g.out, g.come[1])
        pass_on(g, x, high, to_up, g.out, g.near)
        pass_on(g, x, low, to_down, g.out, g.near)
        pass_on(g, x, every, sibling, g.give, g.given)

    def weights_on(g):
        if nx == 2:
            return
        g.far = mark()
        take(span(g, 0, low), g.come[0])
        pass_on(g, down, low, device(x=up), g.out, g.far)
        take(span(g, 0, high), g.come[1])
        pass_on(g, up, high, device(x=down), g.out, g.far)
        pass_on(g, down, low, sibling, g.give, g.given)
        pass_on(g, up, high, sibling, g.give, g.given)

    def weights_last(g):
        take(span(g, 0, every), g.near)
        if nx == 2:
            pass_on(g, up, every, sibling, g.give, g.given)
            return
        pass_on(g, down, high, sibling, g.give, g.given)
        pass_on(g, up, low, sibling, g.give, g.given)
        take(span(g, 0, every), g.far)
        pass_on(g, ahead(x, 2, nx), every, sibling, g.give, g.given)

    for copy in small:
        copy.wait()
    one, two = teams
    (a0, b0), (a1, b1) = one.parts, two.parts
    first_step(a0)
    first_step(b0)
    first_step(a1)
    first_step(b1)
    second_step(a0)
    second_step(b0)
    state_first()
    t = step_ref[0]
    fix_one = 1.0 - power(0.9, t)
    fix_two = 1.0 - power(0.95, t)
    second_step(a1)
    second_step(b1)
    third_step(a0)
    third_step(b0)
    state_second()
    third_step(a1)
    third_step(b1)
    sum_z(one)
    sum_z(two)
    state_done()
    update(one, fix_one, fix_two)
    update(two, fix_one, fix_two)
    weights_y(one)
    masters_z(one)
    weights_y(two)
    masters_z(two)
    weights_x(one)
    weights_x(two)
    pairs_y(one)
    weights_on(one)
    pairs_y(two)
    weights_on(two)
    weights_last(one)
    weights_last(two)
    for g in teams:
        pairs_done(g)
        take(span(g, pl.ds(0, nx), every), g.given)
    finish()


def spread_kernel(dims, new_in, gathered, pairs, master_out, first_out, second_out, weights_out, new_ref, sem):
    nx, ny, nzh, _, _ = dims
    order = pltpu.make_async_copy(new_in, new_ref, sem.at[0])
    order.start()
    copies = []
    for a, ref in enumerate((master_out, first_out, second_out)):
        copies.append(pltpu.make_async_copy(pairs.at[a], ref, sem.at[1 + a]))
        copies[-1].start()
    order.wait()
    for k in range(nzh * nx * ny):
        e, at_x, at_y = k // (nx * ny), k // ny % nx, k % ny
        copy = (
            pltpu.make_async_copy(gathered.at[(at_x * ny + at_y) * nzh + e], weights_out.at[new_ref[k]], sem.at[4])
        )
        copy.start()
    for copy in copies:
        copy.wait()
    pltpu.make_async_copy(gathered, gathered, sem.at[4]).wait()


def step_call(dims, groups, stop, old_order, new_order, step, grads, master, first, second):
    nx, ny, nzh, nzl, tiles = dims
    nz, ns, nb = nzh * nzl, nzh * nx, ny // 2
    half = tiles * LANES
    blocks = ns * ny
    vmem = pltpu.VMEM
    anywhere = pl.BlockSpec(memory_space=pl.ANY)
    outside = pl.BlockSpec(memory_space=pltpu.HBM)
    inside = pl.BlockSpec(memory_space=pltpu.VMEM)
    buffers, state_width = [], 0
    for chunks in groups:
        for along_x, count_tiles in chunks:
            n1, n2 = (nx, ny) if along_x else (ny, nx)
            size = count_tiles * LANES
            buffers += [
                vmem((8 * blocks, size), BF16),
                vmem((8 * blocks, size), BF16),
                vmem((blocks, 8, size), F32),
                vmem((n1, n2, nzh, 8, size), F32),
                vmem((2, n2 // 2, nzh, 8, size), F32),
                vmem((min(n1 - 1, 2), n2, nzh, 8, size), F32),
                vmem((n2, nzh, 8, size), F32),
                vmem((n2 - 1, nzh, 8, size), F32),
            ]
        group_tiles = sum(n for _, n in chunks)
        size = group_tiles * LANES
        width = -(-group_tiles // nzl) * LANES
        fold = -(-width // (2 * LANES)) * LANES
        state_width += width
        buffers += [
            vmem((nzh, 8, size), F32),
            vmem((nz - 1, 8, width), F32),
            vmem((3, 8, width), F32),
            vmem((nzl, 3, 8, width), F32),
            vmem((16, fold), BF16),
            vmem((nz, 16, fold), BF16),
            vmem((8 * nzh, size), BF16),
            vmem((3, 8, size), F32),
        ]
    gathered, pairs = pl.pallas_call(
        functools.partial(kernel, dims, groups, stop),
        out_shape=(pltpu.VMEM((nx, ny, 8 * nzh, 2 * half), BF16), pltpu.VMEM((3, nb, 8, 2 * half), F32)),
        in_specs=[anywhere] * 3 + [outside] * 4,
        out_specs=[inside] * 2,
        scratch_shapes=[
            pltpu.SMEM((blocks,), jnp.int32),
            pltpu.SMEM((blocks,), jnp.int32),
            pltpu.SMEM((1,), jnp.int32),
            vmem((3, ny, 8, state_width), F32),
            vmem((ns, 8, state_width), F32),
            vmem((ns, 8, state_width), F32),
            vmem((ny, 8, state_width), F32),
            vmem((3, 8, state_width), F32),
            pltpu.SemaphoreType.DMA((MARKS,)),
        ] + buffers,
        compiler_params=pltpu.CompilerParams(
            collective_id=0, has_side_effects=True, vmem_limit_bytes=60 * 1024 * 1024
        ),
        cost_estimate=pl.CostEstimate(flops=4_000_000, bytes_accessed=8_000_000, transcendentals=0),
    )(old_order, new_order, step, grads, master, first, second)
    f32_out = jax.ShapeDtypeStruct((nb, 8, 2 * half), F32)
    return pl.pallas_call(
        functools.partial(spread_kernel, dims),
        out_shape=(f32_out, f32_out, f32_out, jax.ShapeDtypeStruct((blocks, 8, 2 * half), BF16)),
        in_specs=[anywhere, inside, inside],
        out_specs=[anywhere] * 4,
        scratch_shapes=[pltpu.SMEM((blocks,), jnp.int32), pltpu.SemaphoreType.DMA((5,))],
        compiler_params=pltpu.CompilerParams(vmem_limit_bytes=8 * 1024 * 1024),
    )(new_order, gathered.reshape(blocks, 8, 2 * half), pairs)


def body(dims, groups, stop, master_old, moment_one_old, moment_two_old, grads, old_order, new_order, step):
    blocks, rows, columns = grads.shape[2:]
    flat = grads.reshape(blocks * rows, columns)
    master, first, second, weights = step_call(
        dims, groups, stop, old_order, new_order, step, flat, master_old, moment_one_old, moment_two_old
    )
    return master[None], first[None], second[None], weights[None]


GROUPS = (((True, 5), (False, 4)), ((True, 4), (False, 5)))


def solution(mesh, dims=(4, 4, 2, 4, 18), groups=GROUPS, stop=0):
    return jax.shard_map(
        functools.partial(body, dims, groups, stop),
        mesh=mesh,
        in_specs=(
            P("shard", None, None),
            P("shard", None, None),
            P("shard", None, None),
            P("rep", "shard", None, None, None),
            P(),
            P(),
            P(),
        ),
        out_specs=(
            P("rep", "shard", None, None),
            P("rep", "shard", None, None),
            P("rep", "shard", None, None),
            P("rep", None, None, None),
        ),
        check_vma=False,
    )
```

time: 854 us -> 59.8 us (0.07)
  waiting for transfers between devices: 807 us -> 0 us
  Pallas kernels: 0 us -> 58.4 us
  local copies, waits for them, and re-layouts: 16.7 us -> 0.01 us
  between operations: 15 us -> 1.32 us
  other arithmetic: 12 us -> 0 us
    all_gather x4 -> x0, waiting for transfers between devices: 408 us -> none  [the longest x1 112 us: body(): lax.all_gather(moment_two_old, 'shard', axis=0, tiled=True)]
    psum x1 -> x0, waiting for transfers between devices: 260 us -> none  [body(): summed = lax.psum(ordered.astype(jnp.float32), 'rep')]
    reduce_scatter x1 -> x0, waiting for transfers between devices: 136 us -> none  [body(): lax.psum_scatter(summed, 'shard', scatter_dimension=0, tiled=True)]
    pallas_call x0 -> x2, Pallas kernels: none -> 58.4 us  [the longest x1 56.4 us: step_call(): pl.pallas_call(functools.partial(kernel, dims, groups, stop), out_shape=(...]
    gather x6 -> x0, local copies, waits for them, and re-layouts: 15.2 us -> none  [the longest x1 3.77 us: body(): weights = jnp.take(gathered, new_slot_of, axis=0)]
  transfers between devices with their start and end apart: 7 -> 0, of which waited for: 7 -> 0; matrix products, arithmetic and copies ran while one was open for 1% -> 0% of each run, Pallas kernels for 0% -> 0%
where the time goes in v4:
time: 59.8 us; the launch traced here: 59.7 us
  Pallas kernels  58.4 us (98%)
  between operations  1.32 us (2%)
    pallas_call x1, Pallas kernels, step_call(): pl.pallas_call(functools.partial(kernel, dims, groups, stop), out_shape=(...  56.4 us
    pallas_call x1, Pallas kernels, step_call(): pl.pallas_call(functools.partial(spread_kernel, dims), out_shape=(f32_out...  1.97 us

profile of v4, /device:TPU:1, one launch (start us, length us, event | category | flops | bytes accessed | tf_op | source)
XLA Modules:
  0.0 59.7 jit_solution(4410397556596590708)
XLA Ops:
  0.6 0.0 copy-start
  1.3 56.4 %shard_map.102 = (bf16[4,4,16,4608]{3,2,1,0:T(8,128)(2,1)S(1)}, f32[3,2,8,4608]{3,2,1,0:T(8,128)S(1)}) custom-call(s32[32]{0:T(128)} %old_in.1, s32[32]{0:T(128)} %new_in.3, s32[1]{0:T(128)S(6)} %copy.11.step_in, bf16[256,4608]{1,0:T(8,128)(2,1)} %bitcast.7, f32[4,8,4608]{2,1,0:T(8,128)} %master.1, f32[4,8,4608]{2,1,0:T(8,128)} %first.1, f32[4,8,4608]{2,1,0:T(8,128)} %second.1), custom_call_target="tpu_custom_call" | custom-call | flops 4000000 | bytes 8000000 | tf_op jit(solution)/shard_map/pallas_call | solution.py:525
  57.7 0.0 copy-done
  57.7 2.0 %shard_map.103 = (f32[2,8,4608]{2,1,0:T(8,128)}, f32[2,8,4608]{2,1,0:T(8,128)}, f32[2,8,4608]{2,1,0:T(8,128)}, bf16[32,8,4608]{2,1,0:T(8,128)(2,1)}) custom-call(s32[32]{0:T(128)S(1)} %copy-done, bf16[32,8,4608]{2,1,0:T(8,128)(2,1)S(1)} %bitcast.6, f32[3,2,8,4608]{3,2,1,0:T(8,128)S(1)} %get-tuple-element.11.pairs), custom_call_target="tpu_custom_call" | custom-call | tf_op jit(solution)/shard_map/pallas_call | solution.py:547
Async XLA Ops:
  0.6 57.1 %copy-start = (s32[32]{0:T(128)S(1)}, s32[32]{0:T(128)}, u32[]{:S(2)}) copy-start(s32[32]{0:T(128)} %new_in.3) | copy-start | bytes 388

commit v5 on v4

--- a/solution.py
+++ b/solution.py
@@ -11,7 +11,7 @@
 
 MESH = pl.DeviceIdType.MESH
 LANES = 128
-MARKS = 91
+MARKS = 97
 F32 = jnp.float32
 BF16 = jnp.bfloat16
 
@@ -28,7 +28,7 @@
 def kernel(
     dims, groups, stop,
     old_in, new_in, step_in, grads, master, first, second,
-    gathered, pairs,
+    gathered, pairs, new_out,
     old_ref, new_ref, step_ref,
     state, state_out, cand, turn, owned,
     sems, *buffers,
@@ -148,10 +148,12 @@
     pl.semaphore_wait(barrier, len(partners))
 
     swap_send = sends(grads.at[:, pl.ds(0, half)])
-    for g in teams:
+
+    def swap(g):
         for p in g.parts:
             p.swap = mark()
             remote(grads.at[:, pl.ds(theirs + p.at, p.size)], p.sib, sibling, swap_send, p.swap)
+
 
     holds = y < 3
     kind = jnp.where(holds, y, 2)
@@ -318,6 +320,12 @@
             g.result[a] = value
             g.result_z[zl, a] = value
 
+    every = pl.ds(0, ny)
+    up, down = ahead(x, 1, nx), ahead(x, nx - 1, nx)
+
+    def extent(g, of, rows):
+        return gathered.at[of, rows, :, pl.ds(0, g.size)]
+
     def block_place(g, of_x, of_y):
         return gathered.at[of_x, of_y, :, pl.ds(mine + g.at, g.size)]
 
@@ -331,98 +339,98 @@
                     rows = [g.short_z[e * nzl + q, :, :high - low].astype(F32)[top:top + 8] for e in range(nzh)]
                     g.wide[:, starts[q] + low:starts[q] + high] = jnp.concatenate(rows, axis=0).astype(BF16)
         place = block_place(g, x, y)
-        rest = gathered.at[0, pl.ds(0, ny - 1), :, pl.ds(0, g.size)]
-        g.over_y, out = mark(), sends(rest)
+        g.over_y, out = mark(), sends(extent(g, 0, pl.ds(0, ny - 1)))
+        g.out = sends(extent(g, pl.ds(0, 3), every))
+        g.come, g.near, g.far = [mark() for _ in range(4)], mark(), mark()
+        remote(g.wide, place, device(x=up), g.out, g.come[0])
+        remote(g.wide, place, device(x=down), g.out, g.near)
         for d in far(ny):
             remote(g.wide, place, device(y=ahead(y, d, ny)), out, g.over_y)
         g.kept = local(g.wide, place, mark())
 
     def masters_z(g):
+        g.over_zl = [mark() for _ in range(nzl)]
+        landed = sems.at[len(used) - nzl + zl]
         if nzl > 1:
-            g.over_zl, out = mark(), sends(g.result_z.at[pl.ds(0, nzl - 1)])
+            out = sends(g.result_z.at[pl.ds(0, nzl - 1)])
         for d in far(nzl):
-            remote(g.result, g.result_z.at[zl], device(zl=ahead(zl, d, nzl)), out, g.over_zl)
+            remote(g.result, g.result_z.at[zl], device(zl=ahead(zl, d, nzl)), out, landed)
 
     member, row = lax.div(y, nb), lax.rem(y, nb)
 
+    def hand_out(g, q, src, when):
+        at, wide = g.starts[q], g.starts[q + 1] - g.starts[q]
+        src = src.at[:, :, pl.ds(0, wide)]
+        place = pairs.at[:, row, :, pl.ds(mine + g.at + at, wide)]
+        for d in far(ny):
+            remote(src, place, device(y=ahead(y, d, ny), core=member), g.pair_out, g.landed, when)
+        remote(src, place, sibling, g.pair_give, g.landed, jnp.logical_and(when, member != core))
+        within = pltpu.make_async_copy(src, place, g.landed)
+        pl.when(jnp.logical_and(when, member == core))(within.start)
+
+    def pairs_own(g):
+        g.pair_marks = [mark() for _ in range(2 * nb)]
+        g.landed = sems.at[len(used) - 2 * nb + row * 2 + core]
+        g.pair_out = sends(pairs.at[:, 0, :, pl.ds(0, (ny - 1) * g.size)])
+        g.pair_give = sends(g.pair, member != core)
+        for q in range(nzl):
+            hand_out(g, q, g.result, zl == q)
+
     def pairs_y(g):
-        if nzl > 1:
-            take(g.result_z.at[pl.ds(0, nzl - 1)], g.over_zl)
-        starts = g.starts
         for q in range(nzl):
-            for a in range(3):
-                g.pair[a, :, starts[q]:starts[q + 1]] = g.result_z[q, a, :, :starts[q + 1] - starts[q]]
-        place = pairs.at[:, row, :, pl.ds(mine + g.at, g.size)]
-        first_mark = len(used)
-        g.pair_marks = [mark() for _ in range(2 * nb)]
-        landed = sems.at[first_mark + row * 2 + core]
-        for d in far(ny):
-            remote(g.pair, place, device(y=ahead(y, d, ny), core=member), sends(g.pair), landed)
-        remote(g.pair, place, sibling, sends(g.pair, member != core), landed, member != core)
-        within = pltpu.make_async_copy(g.pair, place, landed)
-        pl.when(member == core)(within.start)
+            pl.when(zl != q)(functools.partial(take, g.result_z.at[q], g.over_zl[q]))
+            hand_out(g, q, g.result_z.at[q], zl != q)
 
     def pairs_done(g):
         for k in range(2 * nb):
             take(g.pair, g.pair_marks[k])
 
-    h = ny // 2
-    low, high = pl.ds(0, h), pl.ds(h, h)
-    up, down = ahead(x, 1, nx), ahead(x, nx - 1, nx)
-
     def pass_on(g, of, rows, to, send, recv):
         place = gathered.at[of, rows, :, pl.ds(mine + g.at, g.size)]
         remote(place, place, to, send, recv)
 
-    def span(g, of, rows):
-        return gathered.at[of, rows, :, pl.ds(0, g.size)]
-
-    every = pl.ds(0, ny)
-
     def weights_x(g):
-        take(span(g, 0, pl.ds(0, ny - 1)), g.over_y)
+        to_up, to_down = device(x=up), device(x=down)
+        block = extent(g, 0, 0)
+        rows = [ahead(y, j, ny) for j in range(ny)]
+        take(block, g.come[0])
+        pass_on(g, down, rows[0], to_up, g.out, g.far)
+        take(extent(g, 0, pl.ds(0, ny - 1)), g.over_y)
         g.kept.wait()
-        g.given, g.give = mark(), sends(span(g, pl.ds(0, nx), every))
-        if nx == 2:
-            g.near = mark()
-            pass_on(g, x, every, device(x=up), sends(span(g, 0, every)), g.near)
-            pass_on(g, x, every, sibling, g.give, g.given)
-            return
-        to_up, to_down = device(x=up), device(x=down)
-        g.out = sends(span(g, pl.ds(0, 3), every))
-        g.come = [mark(), mark()]
-        g.near = mark()
-        pass_on(g, x, low, to_up, g.out, g.come[0])
-        pass_on(g, x, high, to_down, g.out, g.come[1])
-        pass_on(g, x, high, to_up, g.out, g.near)
-        pass_on(g, x, low, to_down, g.out, g.near)
+        pass_on(g, x, rows[1], to_up, g.out, g.come[1])
+        pass_on(g, x, rows[2], to_down, g.out, g.come[2])
+        pass_on(g, x, rows[3], to_down, g.out, g.come[3])
+        pass_on(g, x, rows[2], to_up, g.out, g.near)
+        pass_on(g, x, rows[3], to_up, g.out, g.near)
+        pass_on(g, x, rows[1], to_down, g.out, g.near)
+        g.given, g.give = mark(), sends(extent(g, pl.ds(0, nx), every))
         pass_on(g, x, every, sibling, g.give, g.given)
 
     def weights_on(g):
-        if nx == 2:
-            return
-        g.far = mark()
-        take(span(g, 0, low), g.come[0])
-        pass_on(g, down, low, device(x=up), g.out, g.far)
-        take(span(g, 0, high), g.come[1])
-        pass_on(g, up, high, device(x=down), g.out, g.far)
-        pass_on(g, down, low, sibling, g.give, g.given)
-        pass_on(g, up, high, sibling, g.give, g.given)
+        block = extent(g, 0, 0)
+        rows = [ahead(y, j, ny) for j in range(ny)]
+        take(block, g.come[1])
+        pass_on(g, down, rows[1], device(x=up), g.out, g.far)
+        take(block, g.come[2])
+        pass_on(g, up, rows[2], device(x=down), g.out, g.far)
+        take(block, g.come[3])
+        pass_on(g, up, rows[3], device(x=down), g.out, g.far)
 
     def weights_last(g):
-        take(span(g, 0, every), g.near)
-        if nx == 2:
-            pass_on(g, up, every, sibling, g.give, g.given)
-            return
-        pass_on(g, down, high, sibling, g.give, g.given)
-        pass_on(g, up, low, sibling, g.give, g.given)
-        take(span(g, 0, every), g.far)
+        take(extent(g, 0, every), g.near)
+        pass_on(g, down, every, sibling, g.give, g.given)
+        pass_on(g, up, every, sibling, g.give, g.given)
+        take(extent(g, 0, every), g.far)
         pass_on(g, ahead(x, 2, nx), every, sibling, g.give, g.given)
 
     for copy in small:
         copy.wait()
+    for k in range(ns * ny):
+        new_out[k] = new_ref[k]
     one, two = teams
     (a0, b0), (a1, b1) = one.parts, two.parts
+    swap(one)
+    swap(two)
     first_step(a0)
     first_step(b0)
     first_step(a1)
@@ -447,8 +455,10 @@
     update(two, fix_one, fix_two)
     weights_y(one)
     masters_z(one)
+    pairs_own(one)
     weights_y(two)
     masters_z(two)
+    pairs_own(two)
     weights_x(one)
     weights_x(two)
     pairs_y(one)
@@ -459,19 +469,16 @@
     weights_last(two)
     for g in teams:
         pairs_done(g)
-        take(span(g, pl.ds(0, nx), every), g.given)
+        take(extent(g, pl.ds(0, nx), every), g.given)
     finish()
 
 
-def spread_kernel(dims, new_in, gathered, pairs, master_out, first_out, second_out, weights_out, new_ref, sem):
+def spread_kernel(dims, new_ref, gathered, pairs, master_out, first_out, second_out, weights_out, sem):
     nx, ny, nzh, _, _ = dims
-    order = pltpu.make_async_copy(new_in, new_ref, sem.at[0])
-    order.start()
     copies = []
     for a, ref in enumerate((master_out, first_out, second_out)):
         copies.append(pltpu.make_async_copy(pairs.at[a], ref, sem.at[1 + a]))
         copies[-1].start()
-    order.wait()
     for k in range(nzh * nx * ny):
         e, at_x, at_y = k // (nx * ny), k // ny % nx, k % ny
         copy = (
@@ -490,6 +497,7 @@
     blocks = ns * ny
     vmem = pltpu.VMEM
     anywhere = pl.BlockSpec(memory_space=pl.ANY)
+    scalars = pl.BlockSpec(memory_space=pltpu.SMEM)
     outside = pl.BlockSpec(memory_space=pltpu.HBM)
     inside = pl.BlockSpec(memory_space=pltpu.VMEM)
     buffers, state_width = [], 0
@@ -522,11 +530,11 @@
             vmem((8 * nzh, size), BF16),
             vmem((3, 8, size), F32),
         ]
-    gathered, pairs = pl.pallas_call(
+    gathered, pairs, kept = pl.pallas_call(
         functools.partial(kernel, dims, groups, stop),
-        out_shape=(pltpu.VMEM((nx, ny, 8 * nzh, 2 * half), BF16), pltpu.VMEM((3, nb, 8, 2 * half), F32)),
+        out_shape=(pltpu.VMEM((nx, ny, 8 * nzh, 2 * half), BF16), pltpu.VMEM((3, nb, 8, 2 * half), F32), pltpu.SMEM((blocks,), jnp.int32)),
         in_specs=[anywhere] * 3 + [outside] * 4,
-        out_specs=[inside] * 2,
+        out_specs=[inside] * 2 + [scalars],
         scratch_shapes=[
             pltpu.SMEM((blocks,), jnp.int32),
             pltpu.SMEM((blocks,), jnp.int32),
@@ -547,11 +555,11 @@
     return pl.pallas_call(
         functools.partial(spread_kernel, dims),
         out_shape=(f32_out, f32_out, f32_out, jax.ShapeDtypeStruct((blocks, 8, 2 * half), BF16)),
-        in_specs=[anywhere, inside, inside],
+        in_specs=[scalars, inside, inside],
         out_specs=[anywhere] * 4,
-        scratch_shapes=[pltpu.SMEM((blocks,), jnp.int32), pltpu.SemaphoreType.DMA((5,))],
+        scratch_shapes=[pltpu.SemaphoreType.DMA((5,))],
         compiler_params=pltpu.CompilerParams(vmem_limit_bytes=8 * 1024 * 1024),
-    )(new_order, gathered.reshape(blocks, 8, 2 * half), pairs)
+    )(kept, gathered.reshape(blocks, 8, 2 * half), pairs)
 
 
 def body(dims, groups, stop, master_old, moment_one_old, moment_two_old, grads, old_order, new_order, step):
@@ -563,7 +571,7 @@
     return master[None], first[None], second[None], weights[None]
 
 
-GROUPS = (((True, 5), (False, 4)), ((True, 4), (False, 5)))
+GROUPS = (((True, 4), (False, 4)), ((True, 5), (False, 5)))
 
 
 def solution(mesh, dims=(4, 4, 2, 4, 18), groups=GROUPS, stop=0):

time: 59.8 us -> 58 us (0.970)
  Pallas kernels: 58.4 us -> 56.6 us
    pallas_call x1, Pallas kernels: 56.4 us -> 54.9 us  [step_call(): pl.pallas_call(functools.partial(kernel, dims, groups, stop), out_shape=(...]
where the time goes in v5:
time: 58 us; the launch traced here: 57.9 us
  Pallas kernels  56.6 us (98%)
  between operations  1.29 us (2%)
    pallas_call x1, Pallas kernels, step_call(): pl.pallas_call(functools.partial(kernel, dims, groups, stop), out_shape=(...  54.9 us
    pallas_call x1, Pallas kernels, step_call(): pl.pallas_call(functools.partial(spread_kernel, dims), out_shape=(f32_out...  1.72 us

profile of v5, /device:TPU:1, one launch (start us, length us, event | category | flops | bytes accessed | tf_op | source)
XLA Modules:
  0.0 57.9 jit_solution(8849443183713003075)
XLA Ops:
  1.3 54.9 %shard_map.102 = (bf16[4,4,16,4608]{3,2,1,0:T(8,128)(2,1)S(1)}, f32[3,2,8,4608]{3,2,1,0:T(8,128)S(1)}, s32[32]{0:T(128)S(4)}) custom-call(s32[32]{0:T(128)} %old_in.1, s32[32]{0:T(128)} %new_in.1, s32[1]{0:T(128)S(6)} %copy.11.step_in, bf16[256,4608]{1,0:T(8,128)(2,1)} %bitcast.7, f32[4,8,4608]{2,1,0:T(8,128)} %master.1, f32[4,8,4608]{2,1,0:T(8,128)} %first.1, ...), custom_call_target="tpu_custom_call" | custom-call | flops 4000000 | bytes 8000000 | tf_op jit(solution)/shard_map/pallas_call | solution.py:533
  56.2 1.7 %shard_map.103 = (f32[2,8,4608]{2,1,0:T(8,128)}, f32[2,8,4608]{2,1,0:T(8,128)}, f32[2,8,4608]{2,1,0:T(8,128)}, bf16[32,8,4608]{2,1,0:T(8,128)(2,1)}) custom-call(s32[32]{0:T(128)S(4)} %get-tuple-element.11.new_ref, bf16[32,8,4608]{2,1,0:T(8,128)(2,1)S(1)} %bitcast.6, f32[3,2,8,4608]{3,2,1,0:T(8,128)S(1)} %get-tuple-element.13.pairs), custom_call_target="tpu_custom_call" | custom-call | tf_op jit(solution)/shard_map/pallas_call | solution.py:555

commit v6 on v5

--- a/solution.py
+++ b/solution.py
@@ -431,21 +431,21 @@
     (a0, b0), (a1, b1) = one.parts, two.parts
     swap(one)
     swap(two)
+    state_first()
     first_step(a0)
     first_step(b0)
     first_step(a1)
     first_step(b1)
     second_step(a0)
     second_step(b0)
-    state_first()
     t = step_ref[0]
     fix_one = 1.0 - power(0.9, t)
     fix_two = 1.0 - power(0.95, t)
     second_step(a1)
     second_step(b1)
+    state_second()
     third_step(a0)
     third_step(b0)
-    state_second()
     third_step(a1)
     third_step(b1)
     sum_z(one)
@@ -454,11 +454,11 @@
     update(one, fix_one, fix_two)
     update(two, fix_one, fix_two)
     weights_y(one)
+    pairs_own(one)
     masters_z(one)
-    pairs_own(one)
     weights_y(two)
+    pairs_own(two)
     masters_z(two)
-    pairs_own(two)
     weights_x(one)
     weights_x(two)
     pairs_y(one)

time: 58 us -> 57.2 us (0.986)
  Pallas kernels: 56.6 us -> 55.9 us
    pallas_call x1, Pallas kernels: 54.9 us -> 54.1 us  [step_call(): pl.pallas_call(functools.partial(kernel, dims, groups, stop), out_shape=(...]
where the time goes in v6:
time: 57.2 us; the launch traced here: 57.1 us
  Pallas kernels  55.9 us (98%)
  between operations  1.29 us (2%)
    pallas_call x1, Pallas kernels, step_call(): pl.pallas_call(functools.partial(kernel, dims, groups, stop), out_shape=(...  54.1 us
    pallas_call x1, Pallas kernels, step_call(): pl.pallas_call(functools.partial(spread_kernel, dims), out_shape=(f32_out...  1.72 us

profile of v6, /device:TPU:1, one launch (start us, length us, event | category | flops | bytes accessed | tf_op | source)
XLA Modules:
  0.0 57.1 jit_solution(7299867552010524487)
XLA Ops:
  1.3 54.1 %shard_map.102 = (bf16[4,4,16,4608]{3,2,1,0:T(8,128)(2,1)S(1)}, f32[3,2,8,4608]{3,2,1,0:T(8,128)S(1)}, s32[32]{0:T(128)S(4)}) custom-call(s32[32]{0:T(128)} %old_in.1, s32[32]{0:T(128)} %new_in.1, s32[1]{0:T(128)S(6)} %copy.11.step_in, bf16[256,4608]{1,0:T(8,128)(2,1)} %bitcast.7, f32[4,8,4608]{2,1,0:T(8,128)} %master.1, f32[4,8,4608]{2,1,0:T(8,128)} %first.1, ...), custom_call_target="tpu_custom_call" | custom-call | flops 4000000 | bytes 8000000 | tf_op jit(solution)/shard_map/pallas_call | solution.py:533
  55.4 1.7 %shard_map.103 = (f32[2,8,4608]{2,1,0:T(8,128)}, f32[2,8,4608]{2,1,0:T(8,128)}, f32[2,8,4608]{2,1,0:T(8,128)}, bf16[32,8,4608]{2,1,0:T(8,128)(2,1)}) custom-call(s32[32]{0:T(128)S(4)} %get-tuple-element.11.new_ref, bf16[32,8,4608]{2,1,0:T(8,128)(2,1)S(1)} %bitcast.6, f32[3,2,8,4608]{3,2,1,0:T(8,128)S(1)} %get-tuple-element.13.pairs), custom_call_target="tpu_custom_call" | custom-call | tf_op jit(solution)/shard_map/pallas_call | solution.py:555

commit v7 on v6

--- a/solution.py
+++ b/solution.py
@@ -220,7 +220,7 @@
             p.chip[2 * i + 1] = both[8:]
             return carry
 
-        lax.fori_loop(0, ns * ny // 2, add, 0)
+        lax.fori_loop(0, ns * ny // 2, add, 0, unroll=4)
 
     def order(p, lead):
         for inner in range(p.n2):
@@ -342,10 +342,10 @@
         g.over_y, out = mark(), sends(extent(g, 0, pl.ds(0, ny - 1)))
         g.out = sends(extent(g, pl.ds(0, 3), every))
         g.come, g.near, g.far = [mark() for _ in range(4)], mark(), mark()
+        for d in far(ny):
+            remote(g.wide, place, device(y=ahead(y, d, ny)), out, g.over_y)
         remote(g.wide, place, device(x=up), g.out, g.come[0])
         remote(g.wide, place, device(x=down), g.out, g.near)
-        for d in far(ny):
-            remote(g.wide, place, device(y=ahead(y, d, ny)), out, g.over_y)
         g.kept = local(g.wide, place, mark())
 
     def masters_z(g):
@@ -393,8 +393,6 @@
         to_up, to_down = device(x=up), device(x=down)
         block = extent(g, 0, 0)
         rows = [ahead(y, j, ny) for j in range(ny)]
-        take(block, g.come[0])
-        pass_on(g, down, rows[0], to_up, g.out, g.far)
         take(extent(g, 0, pl.ds(0, ny - 1)), g.over_y)
         g.kept.wait()
         pass_on(g, x, rows[1], to_up, g.out, g.come[1])
@@ -409,6 +407,8 @@
     def weights_on(g):
         block = extent(g, 0, 0)
         rows = [ahead(y, j, ny) for j in range(ny)]
+        take(block, g.come[0])
+        pass_on(g, down, rows[0], device(x=up), g.out, g.far)
         take(block, g.come[1])
         pass_on(g, down, rows[1], device(x=up), g.out, g.far)
         take(block, g.come[2])

time: 57.2 us -> 57 us (level)
  no operation moved by 1% of the time
where the time goes in v7:
time: 57 us; the launch traced here: 56.9 us
  Pallas kernels  55.6 us (98%)
  between operations  1.29 us (2%)
    pallas_call x1, Pallas kernels, step_call(): pl.pallas_call(functools.partial(kernel, dims, groups, stop), out_shape=(...  53.9 us
    pallas_call x1, Pallas kernels, step_call(): pl.pallas_call(functools.partial(spread_kernel, dims), out_shape=(f32_out...  1.72 us

profile of v7, /device:TPU:1, one launch (start us, length us, event | category | flops | bytes accessed | tf_op | source)
XLA Modules:
  0.0 56.9 jit_solution(10202141710874365428)
XLA Ops:
  1.3 53.9 %shard_map.102 = (bf16[4,4,16,4608]{3,2,1,0:T(8,128)(2,1)S(1)}, f32[3,2,8,4608]{3,2,1,0:T(8,128)S(1)}, s32[32]{0:T(128)S(4)}) custom-call(s32[32]{0:T(128)} %old_in.1, s32[32]{0:T(128)} %new_in.1, s32[1]{0:T(128)S(6)} %copy.11.step_in, bf16[256,4608]{1,0:T(8,128)(2,1)} %bitcast.7, f32[4,8,4608]{2,1,0:T(8,128)} %master.1, f32[4,8,4608]{2,1,0:T(8,128)} %first.1, ...), custom_call_target="tpu_custom_call" | custom-call | flops 4000000 | bytes 8000000 | tf_op jit(solution)/shard_map/pallas_call | solution.py:533
  55.2 1.7 %shard_map.103 = (f32[2,8,4608]{2,1,0:T(8,128)}, f32[2,8,4608]{2,1,0:T(8,128)}, f32[2,8,4608]{2,1,0:T(8,128)}, bf16[32,8,4608]{2,1,0:T(8,128)(2,1)}) custom-call(s32[32]{0:T(128)S(4)} %get-tuple-element.11.new_ref, bf16[32,8,4608]{2,1,0:T(8,128)(2,1)S(1)} %bitcast.6, f32[3,2,8,4608]{3,2,1,0:T(8,128)S(1)} %get-tuple-element.13.pairs), custom_call_target="tpu_custom_call" | custom-call | tf_op jit(solution)/shard_map/pallas_call | solution.py:555

commit v8 on v7

--- a/solution.py
+++ b/solution.py
@@ -220,7 +220,7 @@
             p.chip[2 * i + 1] = both[8:]
             return carry
 
-        lax.fori_loop(0, ns * ny // 2, add, 0, unroll=4)
+        lax.fori_loop(0, ns * ny // 2, add, 0, unroll=8)
 
     def order(p, lead):
         for inner in range(p.n2):

time: 57 us -> 57 us (level)
  no operation moved by 1% of the time
where the time goes in v8:
time: 57 us; the launch traced here: 56.9 us
  Pallas kernels  55.6 us (98%)
  between operations  1.29 us (2%)
    pallas_call x1, Pallas kernels, step_call(): pl.pallas_call(functools.partial(kernel, dims, groups, stop), out_shape=(...  53.9 us
    pallas_call x1, Pallas kernels, step_call(): pl.pallas_call(functools.partial(spread_kernel, dims), out_shape=(f32_out...  1.72 us

profile of v8, /device:TPU:1, one launch (start us, length us, event | category | flops | bytes accessed | tf_op | source)
XLA Modules:
  0.0 56.9 jit_solution(17322772000661852720)
XLA Ops:
  1.3 53.9 %shard_map.102 = (bf16[4,4,16,4608]{3,2,1,0:T(8,128)(2,1)S(1)}, f32[3,2,8,4608]{3,2,1,0:T(8,128)S(1)}, s32[32]{0:T(128)S(4)}) custom-call(s32[32]{0:T(128)} %old_in.1, s32[32]{0:T(128)} %new_in.1, s32[1]{0:T(128)S(6)} %copy.11.step_in, bf16[256,4608]{1,0:T(8,128)(2,1)} %bitcast.7, f32[4,8,4608]{2,1,0:T(8,128)} %master.1, f32[4,8,4608]{2,1,0:T(8,128)} %first.1, ...), custom_call_target="tpu_custom_call" | custom-call | flops 4000000 | bytes 8000000 | tf_op jit(solution)/shard_map/pallas_call | solution.py:533
  55.2 1.7 %shard_map.103 = (f32[2,8,4608]{2,1,0:T(8,128)}, f32[2,8,4608]{2,1,0:T(8,128)}, f32[2,8,4608]{2,1,0:T(8,128)}, bf16[32,8,4608]{2,1,0:T(8,128)(2,1)}) custom-call(s32[32]{0:T(128)S(4)} %get-tuple-element.11.new_ref, bf16[32,8,4608]{2,1,0:T(8,128)(2,1)S(1)} %bitcast.6, f32[3,2,8,4608]{3,2,1,0:T(8,128)S(1)} %get-tuple-element.13.pairs), custom_call_target="tpu_custom_call" | custom-call | tf_op jit(solution)/shard_map/pallas_call | solution.py:555
